TPU v7x, 32 devices: a whole 2x2x4 slice. The times are simulated.
32 devices in a mesh: fsdp: 16 (over z, y, core), tp: 2 (over x).
Axes of the slice: x: 2, y: 2, z: 4, core: 2. Of those that a mesh axis runs over, the one named last changes fastest.
Arguments:
- images: bfloat16 [16, 256, 6144], P('fsdp', None, 'tp'), may hold values from -6 to 6
- keep_index: int32 [16, 64], P('fsdp'), may hold values from 0 to 255, as said below
- teacher_weight: float32 [6144, 3072], P('fsdp', 'tp'), may hold values from -0.078125 to 0.078125
- student_weight: float32 [6144, 3072], P('fsdp', 'tp'), may hold values from -0.078125 to 0.078125
Outputs:
- teacher_next: float32 [6144, 3072], P('fsdp', 'tp')
- student_grad: float32 [6144, 3072], P('fsdp', 'tp')
Inputs may be any that keep to these rules, and one draw needn't show every extreme that they name: `keep_index`: each image's 64 indices are distinct and increasing.
All inputs are finite; a program needn't handle non-finite values.
Results may differ from a plain program's by a relative error of at most 0.0048.
Values may be sent and summed in bfloat16 or wider, within the bound.
A program may use at most 128 MiB of HBM per device.

v0:
```python
import math

import jax
import jax.numpy as jnp
from jax import lax
from jax.sharding import PartitionSpec as P

D = 6144


def layer_norm(values):
    floats = values.astype(jnp.float32)
    centre = jnp.mean(floats, axis=-1, keepdims=True)
    centred = floats - centre
    spread = jnp.mean(centred * centred, axis=-1, keepdims=True)
    return (centred * lax.rsqrt(spread + 1e-06)).astype(jnp.bfloat16)


def pick_rows(table, index):
    return jax.vmap(lambda block, rows: block[rows])(table, index)


def row_product(features, piece):
    return jnp.dot(features, piece, preferred_element_type=jnp.float32)


def shards(images, keep_index, teacher_weight, student_weight):
    img_count = images.shape[0]
    patch_count = images.shape[1]
    keep_count = keep_index.shape[1]
    columns_dev = teacher_weight.shape[1]
    teacher_next = 0.999 * teacher_weight + (1.0 - 0.999) * student_weight
    teacher_panel = teacher_next.astype(jnp.bfloat16)
    student_panel = student_weight.astype(jnp.bfloat16)
    whole = lax.all_gather(images, "tp", axis=2, tiled=True)
    normed = layer_norm(whole)
    flat_all = normed.reshape(img_count * patch_count, D)
    picked = pick_rows(normed, keep_index).reshape(img_count * keep_count, D)
    teacher_out = row_product(flat_all, lax.all_gather(teacher_panel, "fsdp", axis=0, tiled=True))
    student_out = row_product(picked, lax.all_gather(student_panel, "fsdp", axis=0, tiled=True))
    teacher_out = teacher_out.reshape(img_count, patch_count, columns_dev)
    centre = jnp.mean(teacher_out, axis=1, keepdims=True)
    centred_out = teacher_out - centre
    spread = jnp.mean(centred_out * centred_out, axis=1, keepdims=True)
    target = centred_out * lax.rsqrt(spread + 1e-05)
    target_kept = pick_rows(target, keep_index).reshape(img_count * keep_count, columns_dev)
    total_kept = img_count * keep_count * lax.axis_size("fsdp")
    error = ((student_out - target_kept) * (1.0 / math.sqrt(total_kept))).astype(jnp.bfloat16)
    owned = lax.all_to_all(picked, "fsdp", split_axis=1, concat_axis=0, tiled=True)
    student_grad = lax.dot_general(
        owned,
        lax.all_gather(error, "fsdp", axis=0, tiled=True),
        (((0,), (0,)), ((), ())),
        preferred_element_type=jnp.float32,
    )
    return (teacher_next, student_grad)


def solution(mesh):
    placed = (P("fsdp", None, "tp"), P("fsdp", None), P("fsdp", "tp"), P("fsdp", "tp"))
    return jax.shard_map(
        shards,
        mesh=mesh,
        in_specs=placed,
        out_specs=(P("fsdp", "tp"), P("fsdp", "tp")),
        check_vma=False,
    )
```

profile of v0, /device:TPU:1, one launch (start us, length us, event | category | flops | bytes accessed | tf_op | source)
XLA Modules:
  0.0 332.2 jit_solution(17644997353246659866)
XLA Ops:
  7.2 0.0 all-gather.5.cloned.1.call-start
  7.2 0.7 all-gather.5.cloned.1.call-update
  7.9 0.0 copy-start.2
  7.9 0.0 all-gather.9.cloned.1.call-start
  8.0 5.9 %fusion.9 = (bf16[384,1536]{1,0:T(8,128)(2,1)}, f32[384,1536]{1,0:T(8,128)}, bf16[384,1536]{1,0:T(8,128)(2,1)}) fusion(f32[384,1536]{1,0:T(8,128)} %param.7, f32[384,1536]{1,0:T(8,128)} %param.6), kind=kLoop, calls=%fused_computation.25 | loop fusion | flops 2949120 | bytes 9437184 | tf_op jit(solution)/shard_map/convert_element_type | solution.py:33
  13.8 0.0 all-gather.9.cloned.1.call-update
  13.8 0.0 all-gather.7.cloned.1.call-start
  13.9 0.7 all-gather.7.cloned.1.call-update
  14.6 0.0 all-gather.11.cloned.1.call-start
  14.6 0.0 copy-done.2
  14.7 41.9 %all-gather.5.cloned.1.call-done = bf16[1,256,6144]{2,1,0:T(8,128)(2,1)} async-done(((bf16[1,256,3072]{2,1,0:T(8,128)(2,1)}), bf16[1,256,6144]{2,1,0:T(8,128)(2,1)}) %all-gather.5.cloned.1.call-update) | async-done | bytes 3145744 | tf_op jit(solution)/shard_map/all_gather | solution.py:35
  56.6 0.0 copy-start
  56.6 2.5 convert_reduce_fusion
  59.1 0.3 copy-done
  59.4 1.0 fusion.2
  60.4 1.2 fusion.3
  61.6 3.8 %gather_fusion = bf16[64,6144]{1,0:T(8,128)(2,1)} fusion(bf16[1,256,6144]{2,1,0:T(8,128)(2,1)S(1)} %fusion.3, s32[64]{0:T(128)S(1)} %or_bitcast_fusion), kind=kCustom, calls=%fused_computation | custom fusion | bytes 1573376 | tf_op jit(solution)/shard_map/vmap()/gather | solution.py:20
  65.4 92.8 %all-gather.9.cloned.1.call-done = bf16[6144,1536]{1,0:T(8,128)(2,1)} async-done(((bf16[384,1536]{1,0:T(8,128)(2,1)}), bf16[6144,1536]{1,0:T(8,128)(2,1)}) %all-gather.9.cloned.1.call-update) | async-done | bytes 18874384 | tf_op jit(solution)/shard_map/all_gather | solution.py:39
  158.2 9.0 %fusion.10 = (f32[1536]{0:T(1024)S(1)}, f32[256,1536]{1,0:T(8,128)S(1)}) fusion(bf16[6144,1536]{1,0:T(8,128)(2,1)} %all-gather.9.cloned.1.call-done, bf16[1,256,6144]{2,1,0:T(8,128)(2,1)S(1)} %fusion.3), kind=kOutput, calls=%fused_computation.26 | convolution fusion | flops 4832229888 | bytes 23599104 | tf_op jit(solution)/shard_map/dot_general | solution.py:24
  167.2 0.2 multiply_reduce_fusion
  167.4 0.0 copy-start.1
  167.4 0.2 multiply_bitcast_fusion
  167.7 1.0 gather_fusion.1
  168.6 90.1 %all-gather.7.cloned.1.call-done = bf16[6144,1536]{1,0:T(8,128)(2,1)} async-done(((bf16[384,1536]{1,0:T(8,128)(2,1)}), bf16[6144,1536]{1,0:T(8,128)(2,1)}) %all-gather.7.cloned.1.call-update) | async-done | bytes 18874384 | tf_op jit(solution)/shard_map/all_gather | solution.py:40
  258.8 0.0 copy-done.1
  258.8 10.4 %fusion.7 = bf16[64,1536]{1,0:T(8,128)(2,1)} fusion(f32[64,1536]{1,0:T(8,128)S(1)} %gather_fusion.1, bf16[64,6144]{1,0:T(8,128)(2,1)S(1)} %copy-done.1, bf16[6144,1536]{1,0:T(8,128)(2,1)} %all-gather.7.cloned.1.call-done), kind=kOutput, calls=%fused_computation.13 | convolution fusion | flops 1208254464 | bytes 20250624 | tf_op jit(solution)/shard_map/dot_general | solution.py:24
  269.1 0.0 all-gather.11.cloned.1.call-update
  269.2 0.1 copy.9
  269.3 31.6 %all_to_all.19 = bf16[64,16,384]{2,0,1:T(8,128)(2,1)S(1)} all-to-all(bf16[64,16,384]{2,0,1:T(8,128)(2,1)S(1)} %bitcast.26), channel_id=1, replica_groups=mesh['fsdp'=16,'tp'=2] {'fsdp'}, dimensions={1} | all-to-all | bytes 1572864 | tf_op jit(solution)/shard_map/all_to_all | solution.py:49
  300.9 20.1 %all-gather.11.cloned.1.call-done = bf16[1024,1536]{1,0:T(8,128)(2,1)} async-done(((bf16[64,1536]{1,0:T(8,128)(2,1)}), bf16[1024,1536]{1,0:T(8,128)(2,1)}) %all-gather.11.cloned.1.call-update) | async-done | bytes 3145744 | tf_op jit(solution)/shard_map/all_gather | solution.py:52
  321.0 4.7 %fusion.11 = f32[384,1536]{1,0:T(8,128)} fusion(bf16[1024,384]{1,0:T(8,128)(2,1)S(1)} %bitcast.27, bf16[1024,1536]{1,0:T(8,128)(2,1)} %all-gather.11.cloned.1.call-done), kind=kOutput, calls=%fused_computation.27 | convolution fusion | flops 1207959552 | bytes 6291456 | tf_op jit(solution)/shard_map/dot_general | solution.py:50
  (7 shorter events, 0.0 us)
Async XLA Ops:
  7.2 49.4 %all-gather.5.cloned.1.call-start = ((), (), s32[]{:S(2)}) async-start(), calls=%async_computation.1 | async-start | bytes 4718592 | tf_op jit(solution)/shard_map/all_gather | solution.py:35
  7.9 6.7 %copy-start.2 = (s32[1,64]{1,0:T(1,128)S(1)}, s32[1,64]{1,0:T(1,128)}, u32[]{:S(2)}) copy-start(s32[1,64]{1,0:T(1,128)} %param.5) | copy-start | bytes 772
  7.9 150.3 %all-gather.9.cloned.1.call-start = ((), (), s32[]{:S(2)}) async-start(), calls=%async_computation.3 | async-start | bytes 20054016 | tf_op jit(solution)/shard_map/all_gather | solution.py:39
  13.8 244.9 %all-gather.7.cloned.1.call-start = ((), (), s32[]{:S(2)}) async-start(), calls=%async_computation.2 | async-start | bytes 20054016 | tf_op jit(solution)/shard_map/all_gather | solution.py:40
  14.6 306.4 %all-gather.11.cloned.1.call-start = ((), (), s32[]{:S(2)}) async-start(), calls=%async_computation.4 | async-start | bytes 3342336 | tf_op jit(solution)/shard_map/all_gather | solution.py:52
  56.6 2.8 copy-start
  167.4 91.3 %copy-start.1 = (bf16[64,6144]{1,0:T(8,128)(2,1)S(1)}, bf16[64,6144]{1,0:T(8,128)(2,1)}, u32[]{:S(2)}) copy-start(bf16[64,6144]{1,0:T(8,128)(2,1)} %gather_fusion) | copy-start | bytes 2359300
Sparse Core Ops, SparseCore 0:
  9.5 46.9 all-gather.4
  58.7 99.3 all-gather.8
  159.8 98.9 all-gather.6
  269.3 51.6 all-gather.10
where the time goes:
time: 333 us; the launch traced here: 332 us
  waiting for transfers between devices  246 us (74%)
  blocking collectives  31.6 us (9%)
  matrix products  24.1 us (7%)
  between operations  13.9 us (4%)
  other arithmetic  11 us (3%)
  local copies, waits for them, and re-layouts  5.17 us (2%)
    all_gather x1, waiting for transfers between devices, shards(): lax.all_gather(teacher_panel, 'fsdp', axis=0, tiled=True)  92.8 us
    all_gather x1, waiting for transfers between devices, shards(): lax.all_gather(student_panel, 'fsdp', axis=0, tiled=True)  90.1 us
    all_gather x1, waiting for transfers between devices, shards(): whole = lax.all_gather(images, 'tp', axis=2, tiled=True)  41.9 us
    all_to_all x1, blocking collectives, shards(): lax.all_to_all(picked, 'fsdp', split_axis=1, concat_axis=0, tiled=True)  31.6 us
    all_gather x1, waiting for transfers between devices, shards(): lax.all_gather(error, 'fsdp', axis=0, tiled=True)  20.1 us
    dot_general x2, matrix products, row_product(): return jnp.dot(features, piece, preferred_element_type=jnp.float32)  19.4 us
  transfers between devices with their start and end apart: 4, of which 4 were waited for; matrix products, arithmetic and copies ran while one was open for 8% of the time, Pallas kernels for 0%

commit v1 on v0

--- a/solution.py
+++ b/solution.py
@@ -24,6 +24,16 @@
     return jnp.dot(features, piece, preferred_element_type=jnp.float32)
 
 
+def whole_features(images):
+    if lax.axis_size("tp") != 2:
+        return lax.all_gather(images, "tp", axis=2, tiled=True)
+    other = lax.ppermute(images, "tp", [(0, 1), (1, 0)])
+    first = lax.axis_index("tp") == 0
+    return jnp.concatenate(
+        [jnp.where(first, images, other), jnp.where(first, other, images)], axis=2
+    )
+
+
 def shards(images, keep_index, teacher_weight, student_weight):
     img_count = images.shape[0]
     patch_count = images.shape[1]
@@ -32,12 +42,15 @@
     teacher_next = 0.999 * teacher_weight + (1.0 - 0.999) * student_weight
     teacher_panel = teacher_next.astype(jnp.bfloat16)
     student_panel = student_weight.astype(jnp.bfloat16)
-    whole = lax.all_gather(images, "tp", axis=2, tiled=True)
-    normed = layer_norm(whole)
+    whole_panel = lax.all_gather(teacher_panel, "fsdp", axis=0, tiled=True)
+    normed = layer_norm(whole_features(images))
     flat_all = normed.reshape(img_count * patch_count, D)
     picked = pick_rows(normed, keep_index).reshape(img_count * keep_count, D)
-    teacher_out = row_product(flat_all, lax.all_gather(teacher_panel, "fsdp", axis=0, tiled=True))
-    student_out = row_product(picked, lax.all_gather(student_panel, "fsdp", axis=0, tiled=True))
+    owned = lax.all_to_all(picked, "fsdp", split_axis=1, concat_axis=0, tiled=True)
+    partial = row_product(owned, student_panel).astype(jnp.bfloat16)
+    student_out = lax.psum_scatter(partial, "fsdp", scatter_dimension=0, tiled=True)
+    student_out = student_out.astype(jnp.float32)
+    teacher_out = row_product(flat_all, whole_panel)
     teacher_out = teacher_out.reshape(img_count, patch_count, columns_dev)
     centre = jnp.mean(teacher_out, axis=1, keepdims=True)
     centred_out = teacher_out - centre
@@ -46,7 +59,6 @@
     target_kept = pick_rows(target, keep_index).reshape(img_count * keep_count, columns_dev)
     total_kept = img_count * keep_count * lax.axis_size("fsdp")
     error = ((student_out - target_kept) * (1.0 / math.sqrt(total_kept))).astype(jnp.bfloat16)
-    owned = lax.all_to_all(picked, "fsdp", split_axis=1, concat_axis=0, tiled=True)
     student_grad = lax.dot_general(
         owned,
         lax.all_gather(error, "fsdp", axis=0, tiled=True),

time: 333 us -> 258 us (0.77)
  waiting for transfers between devices: 246 us -> 170 us
  matrix products: 24.1 us -> 17.4 us
  blocking collectives: 31.6 us -> 37.3 us
    all_gather x3 -> x1, waiting for transfers between devices: 225 us -> 27.6 us  [shards(): whole_panel = lax.all_gather(teacher_panel, 'fsdp', axis=0, tiled=True)]
    reduce_scatter x0 -> x1, waiting for transfers between devices: none -> 61.1 us  [shards(): lax.psum_scatter(partial, 'fsdp', scatter_dimension=0, tiled=True)]
    ppermute x0 -> x1, waiting for transfers between devices: none -> 34.2 us  [whole_features(): other = lax.ppermute(images, 'tp', [(0, 1), (1, 0)])]
    all_gather x1, waiting for transfers between devices: 20.1 us -> 46.9 us  [shards(): lax.all_gather(error, 'fsdp', axis=0, tiled=True)]
    dot_general x2, matrix products: 19.4 us -> 12.6 us  [row_product(): return jnp.dot(features, piece, preferred_element_type=jnp.float32)]
    all_to_all x1, blocking collectives: 31.6 us -> 37.3 us  [shards(): lax.all_to_all(picked, 'fsdp', split_axis=1, concat_axis=0, tiled=True)]
  transfers between devices with their start and end apart: 4 -> 4, of which waited for: 4 -> 4; matrix products, arithmetic and copies ran while one was open for 8% -> 9% of each run, Pallas kernels for 0% -> 0%
where the time goes in v1:
time: 258 us
  waiting for transfers between devices  170 us (66%)
  blocking collectives  37.3 us (14%)
  matrix products  17.4 us (7%)
  between operations  13.9 us (5%)
  other arithmetic  9.83 us (4%)
  local copies, waits for them, and re-layouts  7.29 us (3%)
    reduce_scatter x1, waiting for transfers between devices, shards(): lax.psum_scatter(partial, 'fsdp', scatter_dimension=0, tiled=True)  61.1 us
    all_gather x1, waiting for transfers between devices, shards(): lax.all_gather(error, 'fsdp', axis=0, tiled=True)  46.9 us
    all_to_all x1, blocking collectives, shards(): lax.all_to_all(picked, 'fsdp', split_axis=1, concat_axis=0, tiled=True)  37.3 us
    ppermute x1, waiting for transfers between devices, whole_features(): other = lax.ppermute(images, 'tp', [(0, 1), (1, 0)])  34.2 us
    all_gather x1, waiting for transfers between devices, shards(): whole_panel = lax.all_gather(teacher_panel, 'fsdp', axis=0, tiled=True)  27.6 us
    dot_general x2, matrix products, row_product(): return jnp.dot(features, piece, preferred_element_type=jnp.float32)  12.6 us
  transfers between devices with their start and end apart: 4, of which 4 were waited for; matrix products, arithmetic and copies ran while one was open for 9% of the time, Pallas kernels for 0%

profile of v1, /device:TPU:1, one launch (start us, length us, event | category | flops | bytes accessed | tf_op | source)
XLA Modules:
  0.0 257.9 jit_solution(3727241415793431681)
XLA Ops:
  7.2 0.0 copy-start.5
  7.2 0.0 copy-start.8
  7.2 0.0 all-gather.3.cloned.1.call-start
  7.2 4.8 %fusion.13 = (bf16[384,1536]{1,0:T(8,128)(2,1)}, f32[384,1536]{1,0:T(8,128)}) fusion(f32[384,1536]{1,0:T(8,128)} %param.7, f32[384,1536]{1,0:T(8,128)} %param.6), kind=kLoop, calls=%fused_computation.34 | loop fusion | flops 2359296 | bytes 8257536 | tf_op jit(solution)/shard_map/convert_element_type | solution.py:43
  12.1 0.0 all-gather.3.cloned.1.call-update
  12.1 0.0 reduce-scatter.2.cloned.1.call-start
  12.1 0.0 copy-done.5
  12.1 2.1 collective-permute-start
  14.3 0.0 copy-done.8
  14.3 34.2 %collective-permute-done = bf16[1,256,3072]{2,1,0:T(8,128)(2,1)S(1)} collective-permute-done((bf16[1,256,3072]{2,1,0:T(8,128)(2,1)S(1)}, bf16[1,256,3072]{2,1,0:T(8,128)(2,1)S(1)}, u32[]{:S(2)}, u32[]{:S(2)}) %collective-permute-start) | collective-permute-done | bytes 1572896 | tf_op jit(solution)/shard_map/ppermute | solution.py:30
  48.5 0.2 broadcast_select_fusion.1
  48.7 0.0 copy-start
  48.7 0.0 copy-start.2
  48.7 0.5 convert_reduce_fusion
  49.2 1.0 fusion.2
  50.2 0.0 copy-done
  50.2 0.1 copy-done.2
  50.4 1.2 fusion.3
  51.6 3.8 %gather_fusion = bf16[64,6144]{1,0:T(8,128)(2,1)} fusion(bf16[1,256,6144]{2,1,0:T(8,128)(2,1)S(1)} %fusion.3, s32[64]{0:T(128)S(1)} %or_bitcast_fusion), kind=kCustom, calls=%fused_computation | custom fusion | bytes 1573376 | tf_op jit(solution)/shard_map/vmap()/gather | solution.py:20
  55.4 0.0 copy-start.4
  55.4 1.4 copy.9
  56.8 37.3 %all_to_all.19 = bf16[64,16,384]{2,0,1:T(8,128)(2,1)S(1)} all-to-all(bf16[64,16,384]{2,0,1:T(8,128)(2,1)S(1)} %bitcast.24), channel_id=1, replica_groups=mesh['fsdp'=16,'tp'=2] {'fsdp'}, dimensions={1} | all-to-all | bytes 1572864 | tf_op jit(solution)/shard_map/all_to_all | solution.py:49
  94.1 0.0 copy-start.6
  94.1 0.9 copy-done.6
  95.0 0.0 copy-done.4
  95.0 3.5 %convolution_convert_fusion = bf16[1024,1536]{1,0:T(8,128)(2,1)} fusion(bf16[1024,384]{1,0:T(8,128)(2,1)S(1)} %bitcast.25, f32[384,1536]{1,0:T(8,128)S(1)} %copy-done.4), kind=kOutput, calls=%fused_computation.9 | convolution fusion | flops 1210122240 | bytes 6291456 | tf_op jit(solution)/shard_map/dot_general | solution.py:24
  98.5 0.0 copy-start.1
  98.5 0.0 copy-start.3
  98.5 0.0 reduce-scatter.2.cloned.1.call-update
  98.5 0.2 all-gather.5.cloned.1.call-start
  98.8 27.6 %all-gather.3.cloned.1.call-done = bf16[6144,1536]{1,0:T(8,128)(2,1)} async-done(((bf16[384,1536]{1,0:T(8,128)(2,1)}), bf16[6144,1536]{1,0:T(8,128)(2,1)}) %all-gather.3.cloned.1.call-update) | async-done | bytes 18874384 | tf_op jit(solution)/shard_map/all_gather | solution.py:45
  126.3 0.0 copy-done.1
  126.3 0.0 copy-done.3
  126.4 9.2 %fusion.14 = (f32[1536]{0:T(1024)S(1)}, f32[256,1536]{1,0:T(8,128)S(1)}) fusion(bf16[6144,1536]{1,0:T(8,128)(2,1)} %all-gather.3.cloned.1.call-done, bf16[256,3072]{1,0:T(8,128)(2,1)S(1)} %bitcast.22, bf16[256,3072]{1,0:T(8,128)(2,1)S(1)} %bitcast.21, f32[256]{0:T(256)S(1)} %add_rsqrt_fusion.1, f32[256]{0:T(256)S(1)} %broadcast_multiply_fusion.1), kind=kOutput, calls=%fused_computation.35 | convolution fusion | flops 4843239936 | bytes 23601152 | tf_op jit(solution)/shard_map/dot_general | solution.py:24
  135.5 0.2 multiply_reduce_fusion
  135.7 0.0 copy-start.7
  135.8 0.2 multiply_bitcast_fusion
  136.0 1.0 gather_fusion.1
  137.0 61.1 %reduce-scatter.2.cloned.1.call-done = bf16[64,1536]{1,0:T(8,128)(2,1)} async-done(((bf16[1024,1536]{1,0:T(8,128)(2,1)}), bf16[64,1536]{1,0:T(8,128)(2,1)}) %reduce-scatter.2.cloned.1.call-update) | async-done | bytes 196624 | tf_op jit(solution)/shard_map/reduce_scatter | solution.py:51
  198.0 1.7 multiply_convert_fusion.2
  199.7 0.0 all-gather.5.cloned.1.call-update
  199.7 46.9 %all-gather.5.cloned.1.call-done = bf16[1024,1536]{1,0:T(8,128)(2,1)} async-done(((bf16[64,1536]{1,0:T(8,128)(2,1)}), bf16[1024,1536]{1,0:T(8,128)(2,1)}) %all-gather.5.cloned.1.call-update) | async-done | bytes 3145744 | tf_op jit(solution)/shard_map/all_gather | solution.py:64
  246.7 0.0 copy-done.7
  246.7 4.7 %fusion.15 = f32[384,1536]{1,0:T(8,128)} fusion(bf16[1024,384]{1,0:T(8,128)(2,1)S(1)} %bitcast.26, bf16[1024,1536]{1,0:T(8,128)(2,1)} %all-gather.5.cloned.1.call-done), kind=kOutput, calls=%fused_computation.36 | convolution fusion | flops 1207959552 | bytes 6291456 | tf_op jit(solution)/shard_map/dot_general | solution.py:62
  (7 shorter events, 0.1 us)
Async XLA Ops:
  7.2 5.0 %copy-start.5 = (bf16[1,256,3072]{2,1,0:T(8,128)(2,1)S(1)}, bf16[1,256,3072]{2,1,0:T(8,128)(2,1)}, u32[]{:S(2)}) copy-start(bf16[1,256,3072]{2,1,0:T(8,128)(2,1)} %param.4) | copy-start | bytes 4718596
  7.2 7.1 %copy-start.8 = (s32[1,64]{1,0:T(1,128)S(1)}, s32[1,64]{1,0:T(1,128)}, u32[]{:S(2)}) copy-start(s32[1,64]{1,0:T(1,128)} %param.5) | copy-start | bytes 772
  7.2 119.2 %all-gather.3.cloned.1.call-start = ((), (), s32[]{:S(2)}) async-start(), calls=%async_computation.3 | async-start | bytes 20054016 | tf_op jit(solution)/shard_map/all_gather | solution.py:45
  12.1 185.9 %reduce-scatter.2.cloned.1.call-start = ((), (), s32[]{:S(2)}) async-start(), calls=%async_computation.2 | async-start | bytes 3342336 | tf_op jit(solution)/shard_map/reduce_scatter | solution.py:51
  12.1 36.3 %collective-permute-start = (bf16[1,256,3072]{2,1,0:T(8,128)(2,1)S(1)}, bf16[1,256,3072]{2,1,0:T(8,128)(2,1)S(1)}, u32[]{:S(2)}, u32[]{:S(2)}) collective-permute-start(bf16[1,256,3072]{2,1,0:T(8,128)(2,1)S(1)} %copy-done.5), channel_id=1, source_target_pairs={{0,1},{1,0},{2,3},{3,2},{4,5},{5,4},{6,7},{7,6},{8,9},{9,8},{10,11... | collective-permute-start | bytes 4718600 | tf_op jit(solution)/shard_map/ppermute | solution.py:30
  48.7 1.5 copy-start
  48.7 1.7 copy-start.2
  55.4 39.7 %copy-start.4 = (f32[384,1536]{1,0:T(8,128)S(1)}, f32[384,1536]{1,0:T(8,128)}, u32[]{:S(2)}) copy-start(f32[384,1536]{1,0:T(8,128)} %param.7) | copy-start | bytes 7077892
  94.1 1.0 copy-start.6
  98.5 27.9 %copy-start.1 = (bf16[1,256,3072]{2,1,0:T(8,128)(2,1)S(1)}, bf16[1,256,3072]{2,1,0:T(8,128)(2,1)}, u32[]{:S(2)}) copy-start(bf16[1,256,3072]{2,1,0:T(8,128)(2,1)} %copy-done) | copy-start | bytes 4718596
  98.5 27.9 %copy-start.3 = (bf16[1,256,3072]{2,1,0:T(8,128)(2,1)S(1)}, bf16[1,256,3072]{2,1,0:T(8,128)(2,1)}, u32[]{:S(2)}) copy-start(bf16[1,256,3072]{2,1,0:T(8,128)(2,1)} %copy-done.2) | copy-start | bytes 4718596
  98.5 148.1 %all-gather.5.cloned.1.call-start = ((), (), s32[]{:S(2)}) async-start(), calls=%async_computation.4 | async-start | bytes 3342336 | tf_op jit(solution)/shard_map/all_gather | solution.py:64
  135.7 110.9 %copy-start.7 = (bf16[64,16,384]{2,0,1:T(8,128)(2,1)S(1)}, bf16[64,16,384]{2,0,1:T(8,128)(2,1)}, u32[]{:S(2)}) copy-start(bf16[64,16,384]{2,0,1:T(8,128)(2,1)} %copy-done.6) | copy-start | bytes 2359300
Sparse Core Ops, SparseCore 0:
  12.2 114.0 all-gather.2
  130.1 67.8 reduce-scatter.1
  200.9 45.7 all-gather.4

commit v2 on v1

--- a/solution.py
+++ b/solution.py
@@ -1,8 +1,11 @@
+import functools
 import math
 
 import jax
 import jax.numpy as jnp
 from jax import lax
+from jax.experimental import pallas as pl
+from jax.experimental.pallas import tpu as pltpu
 from jax.sharding import PartitionSpec as P
 
 D = 6144
@@ -68,10 +71,330 @@
     return (teacher_next, student_grad)
 
 
+MESH = pl.DeviceIdType.MESH
+LANE_BLOCK = 384
+
+
+def fused(n, total_kept, pick, images, tw, sw, tnext, grad, xbuf, nbuf, sbuf, wt, ws, acc, tsib,
+          pbuf, owned, pf, h1s, h1r, h2s, h2r, h3s, h3r, ebuf, loc, xs, xr, rs, rr, ns, nr,
+          as_, ar, h1ss, h1rs, h2ss, h2rs, h3ss, h3rs, ts, tr, es, er, bs, br):
+    f = lax.axis_index("fsdp")
+    t = lax.axis_index("tp")
+    chips = n // 2
+    zs = chips // 2
+    core = lax.rem(f, 2)
+    other = 1 - core
+    chip = lax.div(f, 2)
+    y = lax.rem(chip, 2)
+    z = lax.div(chip, 2)
+    place = (1 - y) * z + y * (chips - 1 - z)
+    patches = images.shape[0]
+    depth = tw.shape[0]
+    blocks = tw.shape[1] // LANE_BLOCK
+    half = blocks // 2
+    keep = pick.shape[0]
+
+    def chip_at(position):
+        position = lax.rem(position + 2 * chips, chips)
+        back = lax.div(position, zs)
+        return (1 - back) * 2 * position + back * (2 * (chips - 1 - position) + 1)
+
+    sibling = (2 * chip + other, t)
+    ahead = (2 * chip_at(place + 1) + core, t)
+    behind = (2 * chip_at(place - 1) + core, t)
+    route = (ahead, behind)
+
+    def remote(src, dst, send, recv, device):
+        return pltpu.make_async_remote_copy(
+            src_ref=src, dst_ref=dst, send_sem=send, recv_sem=recv,
+            device_id=device, device_id_type=MESH)
+
+    barrier = pltpu.get_barrier_semaphore()
+    for j in range(1, n):
+        pl.semaphore_signal(barrier, inc=1, device_id=(lax.rem(f + j, n), t), device_id_type=MESH)
+    pl.semaphore_signal(barrier, inc=1, device_id=(f, 1 - t), device_id_type=MESH)
+    pl.semaphore_wait(barrier, n)
+
+    x_out = remote(images, xbuf.at[t], xs.at[0], xr.at[0], (f, 1 - t))
+    x_out.start()
+    x_own = pltpu.make_async_copy(images, xbuf.at[t], loc.at[0])
+    x_own.start()
+
+    tile = 32
+
+    @pl.loop(0, depth // tile)
+    def _(i):
+        rows = pl.ds(pl.multiple_of(i * tile, tile), tile)
+        student = sw[rows, :]
+        following = 0.999 * tw[rows, :] + (1.0 - 0.999) * student
+        tnext[rows, :] = following
+        for q in range(blocks):
+            columns = slice(q * LANE_BLOCK, (q + 1) * LANE_BLOCK)
+            wt[q, chip, rows, :] = following[:, columns].astype(jnp.bfloat16)
+            ws[q, rows, :] = student[:, columns].astype(jnp.bfloat16)
+
+    def ring_copy(q, s, source):
+        ref = wt.at[q, source]
+        return remote(ref, ref, rs.at[q, s], rr.at[q, s], route[q // half])
+
+    def source_of(q, s):
+        return chip_at(place - s) if q < half else chip_at(place + s)
+
+    for q in range(blocks):
+        ring_copy(q, 0, chip).start()
+
+    def pump(s):
+        for q in range(blocks):
+            arrived = source_of(q, s + 1)
+            ring_copy(q, s, arrived).wait_recv()
+            if s < chips - 2:
+                ring_copy(q, s + 1, arrived).start()
+
+    acc[...] = jnp.zeros_like(acc)
+
+    def consume(low, high):
+        @pl.loop(low, high)
+        def _(s):
+            @pl.loop(0, blocks)
+            def _(q):
+                way = lax.div(q, half)
+                source = chip_at(place - s + 2 * way * s)
+                panel = wt[q, source]
+                acc[0, q] += jnp.dot(nbuf[core, source], panel, preferred_element_type=jnp.float32)
+                acc[1, q] += jnp.dot(sbuf[source], panel, preferred_element_type=jnp.float32)
+
+    pump(0)
+    pump(1)
+    pump(2)
+
+    x_own.wait()
+    remote(images, xbuf.at[1 - t], xs.at[0], xr.at[0], (f, 1 - t)).wait_recv()
+    features = n * depth
+    per_side = n // 2
+
+    @pl.loop(0, patches // 16)
+    def _(i):
+        rows = pl.ds(pl.multiple_of(i * 16, 16), 16)
+        sides = [xbuf[g, rows, :].astype(jnp.float32) for g in range(2)]
+        centre = sum(jnp.sum(v, axis=1, keepdims=True) for v in sides) * (1.0 / features)
+        sides = [v - centre for v in sides]
+        spread = sum(jnp.sum(v * v, axis=1, keepdims=True) for v in sides) * (1.0 / features)
+        scale = lax.rsqrt(spread + 1e-06)
+        for g in range(2):
+            scaled = (sides[g] * scale).astype(jnp.bfloat16)
+            for j in range(per_side):
+                owner = g * per_side + j
+                nbuf[owner % 2, owner // 2, rows, :] = scaled[:, j * depth:(j + 1) * depth]
+
+    n_out = remote(nbuf.at[other], sbuf, ns.at[0], nr.at[0], sibling)
+    n_out.start()
+
+    @pl.loop(0, chips)
+    def _(c):
+        for k in range(2):
+            pbuf[k, c] = jnp.dot(
+                pick[...], nbuf[k, c], preferred_element_type=jnp.float32).astype(jnp.bfloat16)
+
+    def swap_copy(j, to):
+        return remote(pbuf.at[lax.rem(to, 2), lax.div(to, 2)], owned.at[core, chip],
+                      as_.at[j - 1], ar.at[j - 1], (to, t))
+
+    for j in range(1, n):
+        swap_copy(j, lax.rem(f + j, n)).start()
+    owned[core, chip] = pbuf[core, chip]
+
+    pump(3)
+    n_out.wait_recv()
+    consume(0, 4)
+
+    for j in range(1, n):
+        origin = lax.rem(f + n - j, n)
+        remote(pbuf.at[0, 0], owned.at[lax.rem(origin, 2), lax.div(origin, 2)],
+               as_.at[j - 1], ar.at[j - 1], (origin, t)).wait_recv()
+
+    rows_core = chips * keep
+
+    @pl.loop(0, blocks)
+    def _(q):
+        panel = ws[q]
+        send = jnp.dot(owned[other].reshape(rows_core, depth), panel,
+                       preferred_element_type=jnp.float32)
+        h1s[q] = send.astype(jnp.bfloat16).reshape(zs, 2, keep, LANE_BLOCK)
+        mine = jnp.dot(owned[core].reshape(rows_core, depth), panel,
+                       preferred_element_type=jnp.float32)
+        pf[q] = mine.reshape(zs, 2, keep, LANE_BLOCK)
+
+    h1 = remote(h1s, h1r, h1ss.at[0], h1rs.at[0], sibling)
+    h1.start()
+    pump(4)
+    h1.wait_recv()
+
+    @pl.loop(0, blocks)
+    def _(q):
+        @pl.loop(0, zs)
+        def _(g):
+            h2s[q, g] = (pf[q, g, 1 - y] + h1r[q, g, 1 - y].astype(jnp.float32)).astype(jnp.bfloat16)
+            pf[q, g, y] += h1r[q, g, y].astype(jnp.float32)
+
+    across = (2 * (2 * z + 1 - y) + core, t)
+    h2 = remote(h2s, h2r, h2ss.at[0], h2rs.at[0], across)
+    h2.start()
+    consume(4, 6)
+    pump(5)
+    h2.wait_recv()
+
+    @pl.loop(0, zs)
+    def _(g):
+        @pl.loop(0, blocks)
+        def _(q):
+            value = pf[q, g, y] + h2r[q, g].astype(jnp.float32)
+            pf[q, g, y] = value
+            h3s[g, q] = value.astype(jnp.bfloat16)
+
+    def level_copy(j):
+        to = lax.rem(z + j, zs)
+        return remote(h3s.at[to], h3r.at[j - 1], h3ss.at[j - 1], h3rs.at[j - 1],
+                      (2 * (2 * to + y) + core, t))
+
+    for j in range(1, zs):
+        level_copy(j).start()
+    consume(6, 7)
+    pump(6)
+    consume(7, 8)
+
+    def half_copy(q):
+        return remote(acc.at[1, q], tsib.at[q], ts.at[q], tr.at[q], sibling)
+
+    for q in range(blocks):
+        half_copy(q).start()
+    for j in range(1, zs):
+        level_copy(j).wait_recv()
+
+    for q in range(blocks):
+        half_copy(q).wait_recv()
+        value = acc[0, q] + tsib[q]
+        centre = jnp.sum(value, axis=0, keepdims=True) * (1.0 / patches)
+        value = value - centre
+        spread = jnp.sum(value * value, axis=0, keepdims=True) * (1.0 / patches)
+        target = value * lax.rsqrt(spread + 1e-05)
+        upper = target.astype(jnp.bfloat16)
+        lower = (target - upper.astype(jnp.float32)).astype(jnp.bfloat16)
+        kept = (jnp.dot(pick[...], upper, preferred_element_type=jnp.float32)
+                + jnp.dot(pick[...], lower, preferred_element_type=jnp.float32))
+        student = pf[q, z, y]
+        for j in range(1, zs):
+            student = student + h3r[j - 1, q].astype(jnp.float32)
+        ebuf[core, chip, q] = ((student - kept) * (1.0 / math.sqrt(total_kept))).astype(jnp.bfloat16)
+
+    def error_copy(way, s, source):
+        ref = ebuf.at[core, source, pl.ds(way * half, half)]
+        return remote(ref, ref, es.at[way, s], er.at[way, s], route[way])
+
+    def beside_copy(way, s, source, owner):
+        ref = ebuf.at[owner, source, pl.ds(way * half, half)]
+        return remote(ref, ref, bs.at[way, s], br.at[way, s], sibling)
+
+    def turn(way, s):
+        return chip_at(place - s) if way == 0 else chip_at(place + s)
+
+    for way in range(2):
+        error_copy(way, 0, chip).start()
+    for way in range(2):
+        beside_copy(way, 0, chip, core).start()
+    for s in range(chips - 1):
+        for way in range(2):
+            arrived = turn(way, s + 1)
+            error_copy(way, s, arrived).wait_recv()
+            if s < chips - 2:
+                error_copy(way, s + 1, arrived).start()
+            beside_copy(way, s + 1, arrived, core).start()
+    for s in range(chips):
+        for way in range(2):
+            beside_copy(way, s, turn(way, s), other).wait_recv()
+
+    features_rows = owned[...].reshape(n * keep, depth)
+    for q in range(blocks):
+        errors = ebuf[:, :, q].reshape(n * keep, LANE_BLOCK)
+        grad[:, q * LANE_BLOCK:(q + 1) * LANE_BLOCK] = lax.dot_general(
+            features_rows, errors, (((0,), (0,)), ((), ())), preferred_element_type=jnp.float32)
+
+    x_out.wait_send()
+    n_out.wait_send()
+    h1.wait_send()
+    h2.wait_send()
+    for s in range(chips - 1):
+        for q in range(blocks):
+            ring_copy(q, s, chip).wait_send()
+        for way in range(2):
+            error_copy(way, s, chip).wait_send()
+    for s in range(chips):
+        for way in range(2):
+            beside_copy(way, s, chip, core).wait_send()
+    for j in range(1, n):
+        swap_copy(j, lax.rem(f + j, n)).wait_send()
+    for j in range(1, zs):
+        level_copy(j).wait_send()
+    for q in range(blocks):
+        half_copy(q).wait_send()
+
+
+def fused_shards(images, keep_index, teacher_weight, student_weight):
+    n = lax.axis_size("fsdp")
+    patches, width = images.shape[1:]
+    keep = keep_index.shape[1]
+    depth, columns = teacher_weight.shape
+    chips, zs, blocks = n // 2, n // 4, columns // LANE_BLOCK
+    pick = (keep_index[0][:, None] == jnp.arange(patches)[None, :]).astype(jnp.bfloat16)
+    bf, fl = jnp.bfloat16, jnp.float32
+    dma = pltpu.SemaphoreType.DMA
+    vm = pltpu.VMEM
+    scratch = [
+        vm((2, patches, width), bf),
+        vm((2, chips, patches, depth), bf),
+        vm((chips, patches, depth), bf),
+        vm((blocks, chips, depth, LANE_BLOCK), bf),
+        vm((blocks, depth, LANE_BLOCK), bf),
+        vm((2, blocks, patches, LANE_BLOCK), fl),
+        vm((blocks, patches, LANE_BLOCK), fl),
+        vm((2, chips, keep, depth), bf),
+        vm((2, chips, keep, depth), bf),
+        vm((blocks, zs, 2, keep, LANE_BLOCK), fl),
+        vm((blocks, zs, 2, keep, LANE_BLOCK), bf),
+        vm((blocks, zs, 2, keep, LANE_BLOCK), bf),
+        vm((blocks, zs, keep, LANE_BLOCK), bf),
+        vm((blocks, zs, keep, LANE_BLOCK), bf),
+        vm((zs, blocks, keep, LANE_BLOCK), bf),
+        vm((zs - 1, blocks, keep, LANE_BLOCK), bf),
+        vm((2, chips, blocks, keep, LANE_BLOCK), bf),
+        dma((1,)), dma((1,)), dma((1,)),
+        dma((blocks, chips - 1)), dma((blocks, chips - 1)),
+        dma((1,)), dma((1,)),
+        dma((n - 1,)), dma((n - 1,)),
+        dma((1,)), dma((1,)), dma((1,)), dma((1,)),
+        dma((zs - 1,)), dma((zs - 1,)),
+        dma((blocks,)), dma((blocks,)),
+        dma((2, chips - 1)), dma((2, chips - 1)),
+        dma((2, chips)), dma((2, chips)),
+    ]
+    out = jax.ShapeDtypeStruct((depth, columns), fl)
+    return pl.pallas_call(
+        functools.partial(fused, n, keep * n),
+        out_shape=(out, out),
+        in_specs=[pl.BlockSpec(memory_space=pltpu.VMEM)] * 4,
+        out_specs=(pl.BlockSpec(memory_space=pltpu.VMEM),) * 2,
+        scratch_shapes=scratch,
+        compiler_params=pltpu.CompilerParams(
+            collective_id=0, has_side_effects=True, vmem_limit_bytes=60 * 2**20),
+        cost_estimate=pl.CostEstimate(
+            flops=2 * n * depth * columns * (patches + 2 * keep), bytes_accessed=2**24, transcendentals=0),
+    )(pick, images[0], teacher_weight, student_weight)
+
+
 def solution(mesh):
     placed = (P("fsdp", None, "tp"), P("fsdp", None), P("fsdp", "tp"), P("fsdp", "tp"))
+    fits = mesh.shape["tp"] == 2 and mesh.shape["fsdp"] == 16
     return jax.shard_map(
-        shards,
+        fused_shards if fits else shards,
         mesh=mesh,
         in_specs=placed,
         out_specs=(P("fsdp", "tp"), P("fsdp", "tp")),

time: 258 us -> 177 us (0.69)
  Pallas kernels: 0 us -> 170 us
  waiting for transfers between devices: 170 us -> 0 us
  blocking collectives: 37.3 us -> 0 us
  matrix products: 17.4 us -> 0 us
  between operations: 13.9 us -> 0.65 us
  other arithmetic: 9.83 us -> 1.35 us
    pallas_call x0 -> x1, Pallas kernels: none -> 170 us  [fused_shards(): pl.pallas_call(functools.partial(fused, n, keep * n), out_shape=(out, out...]
    all_gather x2 -> x0, waiting for transfers between devices: 74.5 us -> none  [the longest x1 46.9 us: shards(): lax.all_gather(error, 'fsdp', axis=0, tiled=True)]
    reduce_scatter x1 -> x0, waiting for transfers between devices: 61.1 us -> none  [shards(): lax.psum_scatter(partial, 'fsdp', scatter_dimension=0, tiled=True)]
    all_to_all x1 -> x0, blocking collectives: 37.3 us -> none  [shards(): lax.all_to_all(picked, 'fsdp', split_axis=1, concat_axis=0, tiled=True)]
    ppermute x1 -> x0, waiting for transfers between devices: 34.2 us -> none  [whole_features(): other = lax.ppermute(images, 'tp', [(0, 1), (1, 0)])]
    dot_general x3 -> x0, matrix products: 17.4 us -> none  [the longest x2 12.6 us: row_product(): return jnp.dot(features, piece, preferred_element_type=jnp.float32)]
    convert_element_type x3 -> x1, other arithmetic: 7.71 us -> 1.35 us  [fused_shards(): (keep_index[0][:, None] == jnp.arange(patches)[None, :]).astype(jnp.bfloa...]
    gather x3 -> x0, local copies, waits for them, and re-layouts: 4.77 us -> none  [pick_rows(): return jax.vmap(lambda block, rows: block[rows])(table, index)]
  transfers between devices with their start and end apart: 4 -> 0, of which waited for: 4 -> 0; matrix products, arithmetic and copies ran while one was open for 9% -> 0% of each run, Pallas kernels for 0% -> 0%
where the time goes in v2:
time: 177 us
  Pallas kernels  170 us (96%)
  local copies, waits for them, and re-layouts  4.78 us (3%)
    pallas_call x1, Pallas kernels, fused_shards(): pl.pallas_call(functools.partial(fused, n, keep * n), out_shape=(out, out...  170 us
    unnamed x4, local copies, waits for them, and re-layouts  4.78 us

profile of v2, /device:TPU:1, one launch (start us, length us, event | category | flops | bytes accessed | tf_op | source)
XLA Modules:
  0.0 177.2 jit_solution(13101006970824907494)
XLA Ops:
  0.6 1.3 fusion.pick
  2.0 170.4 %shard_map.59 = (f32[384,1536]{1,0:T(8,128)}, f32[384,1536]{1,0:T(8,128)}) custom-call(bf16[64,256]{1,0:T(8,128)(2,1)} %fusion.pick, bf16[256,3072]{1,0:T(8,128)(2,1)} %bitcast.3, f32[384,1536]{1,0:T(8,128)} %tw.1, f32[384,1536]{1,0:T(8,128)} %sw.1), custom_call_target="tpu_custom_call" | custom-call | flops 7247757312 | bytes 16777216 | tf_op jit(solution)/shard_map/pallas_call | solution.py:380
  172.4 0.0 copy-start
  172.4 3.4 %copy.8 = f32[384,1536]{1,0:T(8,128)} copy(f32[384,1536]{1,0:T(8,128)} %get-tuple-element.4) | data formatting | bytes 4718592
  175.8 0.0 copy-done
  175.8 1.4 copy.9
Async XLA Ops:
  172.4 3.4 %copy-start = (f32[384,1536]{1,0:T(8,128)S(1)}, f32[384,1536]{1,0:T(8,128)}, u32[]{:S(2)}) copy-start(f32[384,1536]{1,0:T(8,128)} %get-tuple-element.5) | copy-start | bytes 7077892

commit v3 on v1

--- a/solution.py
+++ b/solution.py
@@ -1,8 +1,11 @@
+import functools
 import math
 
 import jax
 import jax.numpy as jnp
 from jax import lax
+from jax.experimental import pallas as pl
+from jax.experimental.pallas import tpu as pltpu
 from jax.sharding import PartitionSpec as P
 
 D = 6144
@@ -68,10 +71,401 @@
     return (teacher_next, student_grad)
 
 
+MESH = pl.DeviceIdType.MESH
+LANE_BLOCK = 384
+
+
+def fused(n, total_kept, pick, images, tw, sw, tnext, grad, stat, stat_in, nbuf, xk, wt, ws,
+          pt, os_, or_, ys_, yr_, pb, pxs, owned, turned, pf, h1s, h1r, h2s, h2r, h3s, h3r, ebuf,
+          sts, str_, xs, xr, ls, lr, ps, pr, as_, ar, ss, sr, h1ss, h1rs, h2ss, h2rs, h3ss, h3rs,
+          oss, ors, yss, yrs, zss, zrs, ess, ers, bss, brs):
+    f = lax.axis_index("fsdp")
+    t = lax.axis_index("tp")
+    zs = n // 4
+    side = n // 2
+    z = lax.div(f, 4)
+    spot = lax.rem(f, 4)
+    y = lax.div(spot, 2)
+    core = lax.rem(spot, 2)
+    other = 1 - core
+    patches, width = images.shape
+    depth = tw.shape[0]
+    blocks = tw.shape[1] // LANE_BLOCK
+    keep = pick.shape[0]
+    part = keep // 2
+    sibling = (4 * z + 2 * y + other, t)
+    across = (4 * z + 2 * (1 - y) + core, t)
+    mirror = (f, 1 - t)
+
+    def remote(src, dst, send, recv, device):
+        return pltpu.make_async_remote_copy(
+            src_ref=src, dst_ref=dst, send_sem=send, recv_sem=recv,
+            device_id=device, device_id_type=MESH)
+
+    barrier = pltpu.get_barrier_semaphore()
+    for j in range(1, n):
+        pl.semaphore_signal(barrier, inc=1, device_id=(lax.rem(f + j, n), t), device_id_type=MESH)
+    for j in range(4):
+        pl.semaphore_signal(
+            barrier, inc=1, device_id=(4 * z + lax.rem(spot + j, 4), 1 - t), device_id_type=MESH)
+    pl.semaphore_wait(barrier, n + 3)
+
+    lane = lax.broadcasted_iota(jnp.int32, (16, 128), 1)
+
+    @pl.loop(0, patches // 16)
+    def _(i):
+        rows = pl.ds(pl.multiple_of(i * 16, 16), 16)
+        values = images[rows, :].astype(jnp.float32)
+        centre = jnp.sum(values, axis=1, keepdims=True) * (1.0 / width)
+        values = values - centre
+        spread = jnp.sum(values * values, axis=1, keepdims=True)
+        stat[rows, :] = jnp.where(lane < 64, centre, spread)
+
+    stats = remote(stat, stat_in, sts.at[0], str_.at[0], mirror)
+    stats.start()
+
+    tile = 32
+
+    @pl.loop(0, depth // tile)
+    def _(i):
+        rows = pl.ds(pl.multiple_of(i * tile, tile), tile)
+        student = sw[rows, :]
+        following = 0.999 * tw[rows, :] + (1.0 - 0.999) * student
+        tnext[rows, :] = following
+        for q in range(blocks):
+            columns = slice(q * LANE_BLOCK, (q + 1) * LANE_BLOCK)
+            wt[q, z, rows, :] = following[:, columns].astype(jnp.bfloat16)
+            ws[q, rows, :] = student[:, columns].astype(jnp.bfloat16)
+
+    def line_copy(way, q, i, source, to):
+        ref = wt.at[q, source]
+        return remote(ref, ref, ls.at[way, q, i], lr.at[way, q, i], to)
+
+    down = (f - 4, t)
+    up = (f + 4, t)
+    for q in range(blocks):
+        @pl.when(z > 0)
+        def _():
+            line_copy(0, q, 0, z, down).start()
+
+        @pl.when(z < zs - 1)
+        def _():
+            line_copy(1, q, 0, z, up).start()
+
+    def pump(i, q):
+        @pl.when(z + 1 + i < zs)
+        def _():
+            line_copy(0, q, i, z + 1 + i, sibling).wait_recv()
+            if i < zs - 2:
+                @pl.when(z > 0)
+                def _():
+                    line_copy(0, q, i + 1, z + 1 + i, down).start()
+
+        @pl.when(z - 1 - i >= 0)
+        def _():
+            line_copy(1, q, i, z - 1 - i, sibling).wait_recv()
+            if i < zs - 2:
+                @pl.when(z < zs - 1)
+                def _():
+                    line_copy(1, q, i + 1, z - 1 - i, up).start()
+
+    stats.wait_recv()
+
+    @pl.loop(0, patches // 16)
+    def _(i):
+        rows = pl.ds(pl.multiple_of(i * 16, 16), 16)
+        here, there = stat[rows, :], stat_in[rows, :]
+        centre = (here[:, 0:1] + there[:, 0:1]) * 0.5
+        apart = here[:, 0:1] - there[:, 0:1]
+        spread = (here[:, 64:65] + there[:, 64:65]) * (0.5 / width) + apart * apart * 0.25
+        scaled = ((images[rows, :].astype(jnp.float32) - centre) * lax.rsqrt(spread + 1e-06)).astype(jnp.bfloat16)
+        for j in range(side):
+            nbuf[j % 4 // 2, j % 2, j // 4, rows, :] = scaled[:, j * depth:(j + 1) * depth]
+
+    @pl.loop(0, side // 4)
+    def _(level):
+        for j in range(4):
+            rows = jnp.dot(pick[...], nbuf[j // 2, j % 2, level],
+                           preferred_element_type=jnp.float32).astype(jnp.bfloat16)
+            pb[side * t + 4 * level + j] = rows[:part]
+            pxs[4 * level + j] = rows[part:]
+
+    kept_out = remote(pxs, pb.at[pl.ds(side * t, side)], ps.at[0], pr.at[0], mirror)
+    kept_out.start()
+
+    def feature_copy(plane, j):
+        to = lax.rem(spot + j, 4)
+        return remote(nbuf.at[lax.div(to, 2), lax.rem(to, 2)], xk.at[y, core, pl.ds(2 * t, 2)],
+                      xs.at[plane, j], xr.at[plane, j],
+                      (4 * z + to, t if plane == 0 else 1 - t))
+
+    xk[y, core, pl.ds(2 * t, 2)] = nbuf[y, core]
+    kept_in = remote(pxs, pb.at[pl.ds(side * (1 - t), side)], ps.at[0], pr.at[0], mirror)
+    kept_in.wait_recv()
+
+    def half_of(device):
+        return lax.rem(t + lax.div(device, side), 2)
+
+    def swap_copy(j):
+        to = lax.rem(f + j, n)
+        return remote(pb.at[to], owned.at[half_of(to), core, y, z], as_.at[j - 1], ar.at[j - 1], (to, t))
+
+    mine = half_of(f)
+    for j in range(1, n):
+        swap_copy(j).start()
+    owned[mine, core, y, z] = pb[f]
+    for j in range(1, 4):
+        feature_copy(0, j).start()
+    for j in range(4):
+        feature_copy(1, j).start()
+
+    for q in range(blocks):
+        pump(0, q)
+
+    for j in range(1, n):
+        origin = lax.rem(f + n - j, n)
+        remote(pb.at[0],
+               owned.at[mine, lax.rem(origin, 2), lax.div(lax.rem(origin, 4), 2), lax.div(origin, 4)],
+               as_.at[j - 1], ar.at[j - 1], (origin, t)).wait_recv()
+    halves = remote(owned.at[mine], owned.at[mine], ss.at[0], sr.at[0], mirror)
+    halves.start()
+    remote(owned.at[1 - mine], owned.at[1 - mine], ss.at[0], sr.at[0], mirror).wait_recv()
+
+    split = (2, 2, zs, part, LANE_BLOCK)
+    rows_core = 4 * zs * part
+
+    @pl.loop(0, blocks)
+    def _(q):
+        panel = ws[q]
+        send = jnp.dot(owned[:, other].reshape(rows_core, depth), panel,
+                       preferred_element_type=jnp.float32)
+        h1s[q] = send.astype(jnp.bfloat16).reshape(split)
+        own = jnp.dot(owned[:, core].reshape(rows_core, depth), panel,
+                      preferred_element_type=jnp.float32)
+        pf[q] = own.reshape(split)
+
+    h1 = remote(h1s, h1r, h1ss.at[0], h1rs.at[0], sibling)
+    h1.start()
+    for g in range(2):
+        turned[g] = owned[g].reshape(rows_core, depth).T
+    h1.wait_recv()
+
+    @pl.loop(0, blocks)
+    def _(q):
+        for g in range(2):
+            h2s[q, g] = (pf[q, g, 1 - y] + h1r[q, g, 1 - y].astype(jnp.float32)).astype(jnp.bfloat16)
+            pf[q, g, y] += h1r[q, g, y].astype(jnp.float32)
+
+    h2 = remote(h2s, h2r, h2ss.at[0], h2rs.at[0], across)
+    h2.start()
+
+    for q in range(blocks):
+        pump(1, q)
+    h2.wait_recv()
+
+    @pl.loop(0, zs)
+    def _(level):
+        @pl.loop(0, blocks)
+        def _(q):
+            for g in range(2):
+                value = pf[q, g, y, level] + h2r[q, g, level].astype(jnp.float32)
+                pf[q, g, y, level] = value
+                h3s[level, q, g] = value.astype(jnp.bfloat16)
+
+    def level_copy(j):
+        to = lax.rem(z + j, zs)
+        return remote(h3s.at[to], h3r.at[j - 1], h3ss.at[j - 1], h3rs.at[j - 1], (4 * to + spot, t))
+
+    for j in range(1, zs):
+        level_copy(j).start()
+
+    def feature_wait(plane, j):
+        origin = lax.rem(spot + 4 - j, 4)
+        first = 2 * t if plane == 0 else 2 * (1 - t)
+        remote(nbuf.at[0, 0], xk.at[lax.div(origin, 2), lax.rem(origin, 2), pl.ds(first, 2)],
+               xs.at[plane, j], xr.at[plane, j], sibling).wait_recv()
+
+    for j in range(1, 4):
+        feature_wait(0, j)
+    for j in range(4):
+        feature_wait(1, j)
+
+    def sibling_copy(q):
+        return remote(os_.at[q], or_.at[q], oss.at[q], ors.at[q], sibling)
+
+    def across_copy(q):
+        return remote(ys_.at[q], yr_.at[q], yss.at[q], yrs.at[q], across)
+
+    def error_level(q, j):
+        ref = ebuf.at[q, core, y, z]
+        return remote(ref, ref, zss.at[q, j - 1], zrs.at[q, j - 1], (4 * lax.rem(z + j, zs) + spot, t))
+
+    def error_across(q, row):
+        ref = ebuf.at[q, core, row]
+        return remote(ref, ref, ess.at[q], ers.at[q], across)
+
+    def error_sibling(q, owner):
+        ref = ebuf.at[q, owner]
+        return remote(ref, ref, bss.at[q], brs.at[q], sibling)
+
+    def product(q):
+        if zs > 2:
+            pump(zs - 2, q)
+
+        @pl.loop(0, 2)
+        def _(row):
+            for target, owner in ((os_, other), (pt, core)):
+                total = jnp.dot(xk[row, owner, 0], wt[q, 0], preferred_element_type=jnp.float32)
+                for level in range(1, zs):
+                    total += jnp.dot(xk[row, owner, level], wt[q, level],
+                                     preferred_element_type=jnp.float32)
+                target[q, row] = total
+
+        sibling_copy(q).start()
+
+    def cores_add(q):
+        sibling_copy(q).wait_recv()
+        ys_[q] = (pt[q, 1 - y] + or_[q, 1 - y]).astype(jnp.bfloat16)
+        across_copy(q).start()
+        pt[q, y] += or_[q, y]
+
+    def error_of(q):
+        if q == 0:
+            for j in range(1, zs):
+                level_copy(j).wait_recv()
+        across_copy(q).wait_recv()
+        value = pt[q, y] + yr_[q].astype(jnp.float32)
+        centre = jnp.sum(value, axis=0, keepdims=True) * (1.0 / patches)
+        value = value - centre
+        spread = jnp.sum(value * value, axis=0, keepdims=True) * (1.0 / patches)
+        target = value * lax.rsqrt(spread + 1e-05)
+        upper = target.astype(jnp.bfloat16)
+        lower = (target - upper.astype(jnp.float32)).astype(jnp.bfloat16)
+        kept = (jnp.dot(pick[...], upper, preferred_element_type=jnp.float32)
+                + jnp.dot(pick[...], lower, preferred_element_type=jnp.float32))
+        student = pf[q, :, y, z]
+        for j in range(1, zs):
+            student = student + h3r[j - 1, q].astype(jnp.float32)
+        student = student.reshape(keep, LANE_BLOCK)
+        ebuf[q, core, y, z] = ((student - kept) * (1.0 / math.sqrt(total_kept))).astype(jnp.bfloat16)
+        for j in range(1, zs):
+            error_level(q, j).start()
+
+    def levels_in(q):
+        for j in range(1, zs):
+            ref = ebuf.at[q, core, y, lax.rem(z + zs - j, zs)]
+            remote(ref, ref, zss.at[q, j - 1], zrs.at[q, j - 1], sibling).wait_recv()
+        error_across(q, y).start()
+
+    def across_in(q):
+        error_across(q, 1 - y).wait_recv()
+        error_sibling(q, core).start()
+
+    def finish(q):
+        error_sibling(q, other).wait_recv()
+        total = None
+        for g in range(2):
+            errors = ebuf[q, :, :, :, g * part:(g + 1) * part].reshape(rows_core, LANE_BLOCK)
+            term = jnp.dot(turned[g], errors, preferred_element_type=jnp.float32)
+            total = term if total is None else total + term
+        grad[:, q * LANE_BLOCK:(q + 1) * LANE_BLOCK] = total
+
+    stages = (product, cores_add, error_of, levels_in, across_in, finish)
+    for wave in range(blocks + len(stages) - 1):
+        for lag, stage in enumerate(stages):
+            if 0 <= wave - lag < blocks:
+                stage(wave - lag)
+
+    for copy in (stats, kept_out, halves, h1, h2):
+        copy.wait_send()
+    for q in range(blocks):
+        for i in range(zs - 1):
+            @pl.when((z > 0) & (z + i < zs))
+            def _():
+                line_copy(0, q, i, z, sibling).wait_send()
+
+            @pl.when((z < zs - 1) & (z - i >= 0))
+            def _():
+                line_copy(1, q, i, z, sibling).wait_send()
+        sibling_copy(q).wait_send()
+        across_copy(q).wait_send()
+        for j in range(1, zs):
+            error_level(q, j).wait_send()
+        error_across(q, y).wait_send()
+        error_sibling(q, core).wait_send()
+    for j in range(1, n):
+        swap_copy(j).wait_send()
+    for j in range(1, 4):
+        feature_copy(0, j).wait_send()
+    for j in range(4):
+        feature_copy(1, j).wait_send()
+    for j in range(1, zs):
+        level_copy(j).wait_send()
+
+
+def fused_shards(images, keep_index, teacher_weight, student_weight):
+    n = lax.axis_size("fsdp")
+    patches, width = images.shape[1:]
+    keep = keep_index.shape[1]
+    depth, columns = teacher_weight.shape
+    zs, blocks, part = n // 4, columns // LANE_BLOCK, keep // 2
+    pick = (keep_index[0][:, None] == jnp.arange(patches)[None, :]).astype(jnp.bfloat16)
+    bf, fl = jnp.bfloat16, jnp.float32
+    dma = pltpu.SemaphoreType.DMA
+    vm = pltpu.VMEM
+    scratch = [
+        vm((patches, 128), fl), vm((patches, 128), fl),
+        vm((2, 2, zs // 2, patches, depth), bf),
+        vm((2, 2, zs, patches, depth), bf),
+        vm((blocks, zs, depth, LANE_BLOCK), bf),
+        vm((blocks, depth, LANE_BLOCK), bf),
+        vm((blocks, 2, patches, LANE_BLOCK), fl),
+        vm((blocks, 2, patches, LANE_BLOCK), fl),
+        vm((blocks, 2, patches, LANE_BLOCK), fl),
+        vm((blocks, patches, LANE_BLOCK), bf),
+        vm((blocks, patches, LANE_BLOCK), bf),
+        vm((n, part, depth), bf),
+        vm((n // 2, part, depth), bf),
+        vm((2, 2, 2, zs, part, depth), bf),
+        vm((2, depth, n * part), bf),
+        vm((blocks, 2, 2, zs, part, LANE_BLOCK), fl),
+        vm((blocks, 2, 2, zs, part, LANE_BLOCK), bf),
+        vm((blocks, 2, 2, zs, part, LANE_BLOCK), bf),
+        vm((blocks, 2, zs, part, LANE_BLOCK), bf),
+        vm((blocks, 2, zs, part, LANE_BLOCK), bf),
+        vm((zs, blocks, 2, part, LANE_BLOCK), bf),
+        vm((zs - 1, blocks, 2, part, LANE_BLOCK), bf),
+        vm((blocks, 2, 2, zs, keep, LANE_BLOCK), bf),
+        dma((1,)), dma((1,)),
+        dma((2, 4)), dma((2, 4)),
+        dma((2, blocks, zs - 1)), dma((2, blocks, zs - 1)),
+        dma((1,)), dma((1,)),
+        dma((n - 1,)), dma((n - 1,)),
+        dma((1,)), dma((1,)), dma((1,)), dma((1,)), dma((1,)), dma((1,)),
+        dma((zs - 1,)), dma((zs - 1,)),
+        dma((blocks,)), dma((blocks,)), dma((blocks,)), dma((blocks,)),
+        dma((blocks, zs - 1)), dma((blocks, zs - 1)),
+        dma((blocks,)), dma((blocks,)), dma((blocks,)), dma((blocks,)),
+    ]
+    out = jax.ShapeDtypeStruct((depth, columns), fl)
+    return pl.pallas_call(
+        functools.partial(fused, n, keep * n),
+        out_shape=(out, out),
+        in_specs=[pl.BlockSpec(memory_space=pltpu.VMEM)] * 4,
+        out_specs=(pl.BlockSpec(memory_space=pltpu.VMEM),) * 2,
+        scratch_shapes=scratch,
+        compiler_params=pltpu.CompilerParams(
+            collective_id=0, has_side_effects=True, vmem_limit_bytes=60 * 2**20),
+        cost_estimate=pl.CostEstimate(
+            flops=2 * n * depth * columns * (patches + 2 * keep), bytes_accessed=2**24, transcendentals=0),
+    )(pick, images[0], teacher_weight, student_weight)
+
+
 def solution(mesh):
     placed = (P("fsdp", None, "tp"), P("fsdp", None), P("fsdp", "tp"), P("fsdp", "tp"))
+    fits = mesh.shape["tp"] == 2 and mesh.shape["fsdp"] == 16
     return jax.shard_map(
-        shards,
+        fused_shards if fits else shards,
         mesh=mesh,
         in_specs=placed,
         out_specs=(P("fsdp", "tp"), P("fsdp", "tp")),

time: 258 us -> 156 us (0.60)
  waiting for transfers between devices: 170 us -> 0 us
  Pallas kernels: 0 us -> 149 us
  blocking collectives: 37.3 us -> 0 us
  matrix products: 17.4 us -> 0 us
  between operations: 13.9 us -> 0.65 us
  other arithmetic: 9.83 us -> 1.35 us
    pallas_call x0 -> x1, Pallas kernels: none -> 149 us  [fused_shards(): pl.pallas_call(functools.partial(fused, n, keep * n), out_shape=(out, out...]
    all_gather x2 -> x0, waiting for transfers between devices: 74.5 us -> none  [the longest x1 46.9 us: shards(): lax.all_gather(error, 'fsdp', axis=0, tiled=True)]
    reduce_scatter x1 -> x0, waiting for transfers between devices: 61.1 us -> none  [shards(): lax.psum_scatter(partial, 'fsdp', scatter_dimension=0, tiled=True)]
    all_to_all x1 -> x0, blocking collectives: 37.3 us -> none  [shards(): lax.all_to_all(picked, 'fsdp', split_axis=1, concat_axis=0, tiled=True)]
    ppermute x1 -> x0, waiting for transfers between devices: 34.2 us -> none  [whole_features(): other = lax.ppermute(images, 'tp', [(0, 1), (1, 0)])]
    dot_general x3 -> x0, matrix products: 17.4 us -> none  [the longest x2 12.6 us: row_product(): return jnp.dot(features, piece, preferred_element_type=jnp.float32)]
    convert_element_type x3 -> x1, other arithmetic: 7.71 us -> 1.35 us  [fused_shards(): (keep_index[0][:, None] == jnp.arange(patches)[None, :]).astype(jnp.bfloa...]
    gather x3 -> x0, local copies, waits for them, and re-layouts: 4.77 us -> none  [pick_rows(): return jax.vmap(lambda block, rows: block[rows])(table, index)]
  transfers between devices with their start and end apart: 4 -> 0, of which waited for: 4 -> 0; matrix products, arithmetic and copies ran while one was open for 9% -> 0% of each run, Pallas kernels for 0% -> 0%
where the time goes in v3:
time: 156 us; the launch traced here: 155 us
  Pallas kernels  149 us (96%)
  local copies, waits for them, and re-layouts  4.78 us (3%)
    pallas_call x1, Pallas kernels, fused_shards(): pl.pallas_call(functools.partial(fused, n, keep * n), out_shape=(out, out...  149 us
    unnamed x4, local copies, waits for them, and re-layouts  4.78 us

profile of v3, /device:TPU:1, one launch (start us, length us, event | category | flops | bytes accessed | tf_op | source)
XLA Modules:
  0.0 155.3 jit_solution(5855519894912206117)
XLA Ops:
  0.6 1.3 fusion.pick
  2.0 148.5 %shard_map.59 = (f32[384,1536]{1,0:T(8,128)}, f32[384,1536]{1,0:T(8,128)}) custom-call(bf16[64,256]{1,0:T(8,128)(2,1)} %fusion.pick, bf16[256,3072]{1,0:T(8,128)(2,1)} %bitcast.3, f32[384,1536]{1,0:T(8,128)} %tw.1, f32[384,1536]{1,0:T(8,128)} %sw.1), custom_call_target="tpu_custom_call" | custom-call | flops 7247757312 | bytes 16777216 | tf_op jit(solution)/shard_map/pallas_call | solution.py:451
  150.5 0.0 copy-start
  150.5 3.4 %copy.8 = f32[384,1536]{1,0:T(8,128)} copy(f32[384,1536]{1,0:T(8,128)} %get-tuple-element.4) | data formatting | bytes 4718592
  153.9 0.0 copy-done
  153.9 1.4 copy.9
Async XLA Ops:
  150.5 3.4 %copy-start = (f32[384,1536]{1,0:T(8,128)S(1)}, f32[384,1536]{1,0:T(8,128)}, u32[]{:S(2)}) copy-start(f32[384,1536]{1,0:T(8,128)} %get-tuple-element.5) | copy-start | bytes 7077892

commit v4 on v3

--- a/solution.py
+++ b/solution.py
@@ -72,13 +72,13 @@
 
 
 MESH = pl.DeviceIdType.MESH
-LANE_BLOCK = 384
-
-
-def fused(n, total_kept, pick, images, tw, sw, tnext, grad, stat, stat_in, nbuf, xk, wt, ws,
+LANE_BLOCK = 256
+
+
+def fused(n, total_kept, pick, images_hbm, tw_hbm, sw_hbm, tnext_hbm, grad_hbm, images, tw, sw, tnext, grad, stat, stat_in, nbuf, xk, wt, ws,
           pt, os_, or_, ys_, yr_, pb, pxs, owned, turned, pf, h1s, h1r, h2s, h2r, h3s, h3r, ebuf,
           sts, str_, xs, xr, ls, lr, ps, pr, as_, ar, ss, sr, h1ss, h1rs, h2ss, h2rs, h3ss, h3rs,
-          oss, ors, yss, yrs, zss, zrs, ess, ers, bss, brs):
+          oss, ors, yss, yrs, zss, zrs, ess, ers, bss, brs, loads, stores):
     f = lax.axis_index("fsdp")
     t = lax.axis_index("tp")
     zs = n // 4
@@ -102,6 +102,11 @@
             src_ref=src, dst_ref=dst, send_sem=send, recv_sem=recv,
             device_id=device, device_id_type=MESH)
 
+    fetched = [pltpu.make_async_copy(a, b, loads.at[i])
+               for i, (a, b) in enumerate(((tw_hbm, tw), (sw_hbm, sw), (images_hbm, images)))]
+    for copy in fetched:
+        copy.start()
+
     barrier = pltpu.get_barrier_semaphore()
     for j in range(1, n):
         pl.semaphore_signal(barrier, inc=1, device_id=(lax.rem(f + j, n), t), device_id_type=MESH)
@@ -110,6 +115,39 @@
             barrier, inc=1, device_id=(4 * z + lax.rem(spot + j, 4), 1 - t), device_id_type=MESH)
     pl.semaphore_wait(barrier, n + 3)
 
+    def line_copy(way, q, i, source, to):
+        ref = wt.at[q, source]
+        return remote(ref, ref, ls.at[way, q, i], lr.at[way, q, i], to)
+
+    down = (f - 4, t)
+    up = (f + 4, t)
+    tile = 64
+    fetched[0].wait()
+    fetched[1].wait()
+    for q in range(blocks):
+        columns = slice(q * LANE_BLOCK, (q + 1) * LANE_BLOCK)
+
+        @pl.loop(0, depth // tile)
+        def _(i):
+            rows = pl.ds(pl.multiple_of(i * tile, tile), tile)
+            student = sw[rows, columns]
+            following = 0.999 * tw[rows, columns] + (1.0 - 0.999) * student
+            tnext[rows, columns] = following
+            wt[q, z, rows, :] = following.astype(jnp.bfloat16)
+            ws[q, rows, :] = student.astype(jnp.bfloat16)
+
+        @pl.when(z > 0)
+        def _():
+            line_copy(0, q, 0, z, down).start()
+
+        @pl.when(z < zs - 1)
+        def _():
+            line_copy(1, q, 0, z, up).start()
+
+    next_out = pltpu.make_async_copy(tnext, tnext_hbm, stores.at[blocks])
+    next_out.start()
+
+    fetched[2].wait()
     lane = lax.broadcasted_iota(jnp.int32, (16, 128), 1)
 
     @pl.loop(0, patches // 16)
@@ -123,34 +161,6 @@
 
     stats = remote(stat, stat_in, sts.at[0], str_.at[0], mirror)
     stats.start()
-
-    tile = 32
-
-    @pl.loop(0, depth // tile)
-    def _(i):
-        rows = pl.ds(pl.multiple_of(i * tile, tile), tile)
-        student = sw[rows, :]
-        following = 0.999 * tw[rows, :] + (1.0 - 0.999) * student
-        tnext[rows, :] = following
-        for q in range(blocks):
-            columns = slice(q * LANE_BLOCK, (q + 1) * LANE_BLOCK)
-            wt[q, z, rows, :] = following[:, columns].astype(jnp.bfloat16)
-            ws[q, rows, :] = student[:, columns].astype(jnp.bfloat16)
-
-    def line_copy(way, q, i, source, to):
-        ref = wt.at[q, source]
-        return remote(ref, ref, ls.at[way, q, i], lr.at[way, q, i], to)
-
-    down = (f - 4, t)
-    up = (f + 4, t)
-    for q in range(blocks):
-        @pl.when(z > 0)
-        def _():
-            line_copy(0, q, 0, z, down).start()
-
-        @pl.when(z < zs - 1)
-        def _():
-            line_copy(1, q, 0, z, up).start()
 
     def pump(i, q):
         @pl.when(z + 1 + i < zs)
@@ -216,10 +226,10 @@
     owned[mine, core, y, z] = pb[f]
     for j in range(1, 4):
         feature_copy(0, j).start()
-    for j in range(4):
+    for j in range(2):
         feature_copy(1, j).start()
 
-    for q in range(blocks):
+    for q in range(blocks // 2):
         pump(0, q)
 
     for j in range(1, n):
@@ -229,10 +239,24 @@
                as_.at[j - 1], ar.at[j - 1], (origin, t)).wait_recv()
     halves = remote(owned.at[mine], owned.at[mine], ss.at[0], sr.at[0], mirror)
     halves.start()
+    for j in range(2, 4):
+        feature_copy(1, j).start()
+    for q in range(blocks // 2, blocks):
+        pump(0, q)
     remote(owned.at[1 - mine], owned.at[1 - mine], ss.at[0], sr.at[0], mirror).wait_recv()
 
     split = (2, 2, zs, part, LANE_BLOCK)
     rows_core = 4 * zs * part
+
+    def h1_copy(q):
+        return remote(h1s.at[q], h1r.at[q], h1ss.at[q], h1rs.at[q], sibling)
+
+    def h2_copy(q):
+        return remote(h2s.at[q], h2r.at[q], h2ss.at[q], h2rs.at[q], across)
+
+    def level_copy(q, j):
+        to = lax.rem(z + j, zs)
+        return remote(h3s.at[q, to], h3r.at[q, j - 1], h3ss.at[q, j - 1], h3rs.at[q, j - 1], (4 * to + spot, t))
 
     @pl.loop(0, blocks)
     def _(q):
@@ -240,44 +264,35 @@
         send = jnp.dot(owned[:, other].reshape(rows_core, depth), panel,
                        preferred_element_type=jnp.float32)
         h1s[q] = send.astype(jnp.bfloat16).reshape(split)
+        h1_copy(q).start()
         own = jnp.dot(owned[:, core].reshape(rows_core, depth), panel,
                       preferred_element_type=jnp.float32)
         pf[q] = own.reshape(split)
 
-    h1 = remote(h1s, h1r, h1ss.at[0], h1rs.at[0], sibling)
-    h1.start()
-    for g in range(2):
-        turned[g] = owned[g].reshape(rows_core, depth).T
-    h1.wait_recv()
-
     @pl.loop(0, blocks)
     def _(q):
+        h1_copy(q).wait_recv()
         for g in range(2):
             h2s[q, g] = (pf[q, g, 1 - y] + h1r[q, g, 1 - y].astype(jnp.float32)).astype(jnp.bfloat16)
             pf[q, g, y] += h1r[q, g, y].astype(jnp.float32)
-
-    h2 = remote(h2s, h2r, h2ss.at[0], h2rs.at[0], across)
-    h2.start()
+        h2_copy(q).start()
+
+    for g in range(2):
+        turned[g] = owned[g].reshape(rows_core, depth).T
 
     for q in range(blocks):
         pump(1, q)
-    h2.wait_recv()
-
-    @pl.loop(0, zs)
-    def _(level):
-        @pl.loop(0, blocks)
-        def _(q):
+        h2_copy(q).wait_recv()
+
+        @pl.loop(0, zs)
+        def _(level):
             for g in range(2):
                 value = pf[q, g, y, level] + h2r[q, g, level].astype(jnp.float32)
                 pf[q, g, y, level] = value
-                h3s[level, q, g] = value.astype(jnp.bfloat16)
-
-    def level_copy(j):
-        to = lax.rem(z + j, zs)
-        return remote(h3s.at[to], h3r.at[j - 1], h3ss.at[j - 1], h3rs.at[j - 1], (4 * to + spot, t))
-
-    for j in range(1, zs):
-        level_copy(j).start()
+                h3s[q, level, g] = value.astype(jnp.bfloat16)
+
+        for j in range(1, zs):
+            level_copy(q, j).start()
 
     def feature_wait(plane, j):
         origin = lax.rem(spot + 4 - j, 4)
@@ -330,9 +345,8 @@
         pt[q, y] += or_[q, y]
 
     def error_of(q):
-        if q == 0:
-            for j in range(1, zs):
-                level_copy(j).wait_recv()
+        for j in range(1, zs):
+            level_copy(q, j).wait_recv()
         across_copy(q).wait_recv()
         value = pt[q, y] + yr_[q].astype(jnp.float32)
         centre = jnp.sum(value, axis=0, keepdims=True) * (1.0 / patches)
@@ -345,7 +359,7 @@
                 + jnp.dot(pick[...], lower, preferred_element_type=jnp.float32))
         student = pf[q, :, y, z]
         for j in range(1, zs):
-            student = student + h3r[j - 1, q].astype(jnp.float32)
+            student = student + h3r[q, j - 1].astype(jnp.float32)
         student = student.reshape(keep, LANE_BLOCK)
         ebuf[q, core, y, z] = ((student - kept) * (1.0 / math.sqrt(total_kept))).astype(jnp.bfloat16)
         for j in range(1, zs):
@@ -369,15 +383,21 @@
             term = jnp.dot(turned[g], errors, preferred_element_type=jnp.float32)
             total = term if total is None else total + term
         grad[:, q * LANE_BLOCK:(q + 1) * LANE_BLOCK] = total
-
-    stages = (product, cores_add, error_of, levels_in, across_in, finish)
-    for wave in range(blocks + len(stages) - 1):
-        for lag, stage in enumerate(stages):
+        grad_copy(q).start()
+
+    def grad_copy(q):
+        columns = pl.ds(q * LANE_BLOCK, LANE_BLOCK)
+        return pltpu.make_async_copy(grad.at[:, columns], grad_hbm.at[:, columns], stores.at[q])
+
+    stages = ((product, 0), (error_of, 1), (cores_add, 0), (levels_in, 2), (across_in, 3), (finish, 4))
+    for wave in range(blocks + 4):
+        for stage, lag in stages:
             if 0 <= wave - lag < blocks:
                 stage(wave - lag)
 
-    for copy in (stats, kept_out, halves, h1, h2):
+    for copy in (stats, kept_out, halves):
         copy.wait_send()
+    next_out.wait()
     for q in range(blocks):
         for i in range(zs - 1):
             @pl.when((z > 0) & (z + i < zs))
@@ -387,9 +407,13 @@
             @pl.when((z < zs - 1) & (z - i >= 0))
             def _():
                 line_copy(1, q, i, z, sibling).wait_send()
+        grad_copy(q).wait()
+        h1_copy(q).wait_send()
+        h2_copy(q).wait_send()
         sibling_copy(q).wait_send()
         across_copy(q).wait_send()
         for j in range(1, zs):
+            level_copy(q, j).wait_send()
             error_level(q, j).wait_send()
         error_across(q, y).wait_send()
         error_sibling(q, core).wait_send()
@@ -399,8 +423,6 @@
         feature_copy(0, j).wait_send()
     for j in range(4):
         feature_copy(1, j).wait_send()
-    for j in range(1, zs):
-        level_copy(j).wait_send()
 
 
 def fused_shards(images, keep_index, teacher_weight, student_weight):
@@ -414,6 +436,8 @@
     dma = pltpu.SemaphoreType.DMA
     vm = pltpu.VMEM
     scratch = [
+        vm((patches, width), bf), vm((depth, columns), fl), vm((depth, columns), fl),
+        vm((depth, columns), fl), vm((depth, columns), fl),
         vm((patches, 128), fl), vm((patches, 128), fl),
         vm((2, 2, zs // 2, patches, depth), bf),
         vm((2, 2, zs, patches, depth), bf),
@@ -433,26 +457,28 @@
         vm((blocks, 2, 2, zs, part, LANE_BLOCK), bf),
         vm((blocks, 2, zs, part, LANE_BLOCK), bf),
         vm((blocks, 2, zs, part, LANE_BLOCK), bf),
-        vm((zs, blocks, 2, part, LANE_BLOCK), bf),
-        vm((zs - 1, blocks, 2, part, LANE_BLOCK), bf),
+        vm((blocks, zs, 2, part, LANE_BLOCK), bf),
+        vm((blocks, zs - 1, 2, part, LANE_BLOCK), bf),
         vm((blocks, 2, 2, zs, keep, LANE_BLOCK), bf),
         dma((1,)), dma((1,)),
         dma((2, 4)), dma((2, 4)),
         dma((2, blocks, zs - 1)), dma((2, blocks, zs - 1)),
         dma((1,)), dma((1,)),
         dma((n - 1,)), dma((n - 1,)),
-        dma((1,)), dma((1,)), dma((1,)), dma((1,)), dma((1,)), dma((1,)),
-        dma((zs - 1,)), dma((zs - 1,)),
+        dma((1,)), dma((1,)),
         dma((blocks,)), dma((blocks,)), dma((blocks,)), dma((blocks,)),
         dma((blocks, zs - 1)), dma((blocks, zs - 1)),
         dma((blocks,)), dma((blocks,)), dma((blocks,)), dma((blocks,)),
+        dma((blocks, zs - 1)), dma((blocks, zs - 1)),
+        dma((blocks,)), dma((blocks,)), dma((blocks,)), dma((blocks,)),
+        dma((3,)), dma((blocks + 1,)),
     ]
     out = jax.ShapeDtypeStruct((depth, columns), fl)
     return pl.pallas_call(
         functools.partial(fused, n, keep * n),
         out_shape=(out, out),
-        in_specs=[pl.BlockSpec(memory_space=pltpu.VMEM)] * 4,
-        out_specs=(pl.BlockSpec(memory_space=pltpu.VMEM),) * 2,
+        in_specs=[pl.BlockSpec(memory_space=pltpu.VMEM)] + [pl.BlockSpec(memory_space=pl.ANY)] * 3,
+        out_specs=(pl.BlockSpec(memory_space=pl.ANY),) * 2,
         scratch_shapes=scratch,
         compiler_params=pltpu.CompilerParams(
             collective_id=0, has_side_effects=True, vmem_limit_bytes=60 * 2**20),

time: 156 us -> 147 us (0.942)
  Pallas kernels: 149 us -> 140 us
    pallas_call x1, Pallas kernels: 149 us -> 140 us  [fused_shards(): pl.pallas_call(functools.partial(fused, n, keep * n), out_shape=(out, out...]
where the time goes in v4:
time: 147 us
  Pallas kernels  140 us (95%)
  local copies, waits for them, and re-layouts  4.78 us (3%)
    pallas_call x1, Pallas kernels, fused_shards(): pl.pallas_call(functools.partial(fused, n, keep * n), out_shape=(out, out...  140 us
    unnamed x4, local copies, waits for them, and re-layouts  4.78 us

profile of v4, /device:TPU:1, one launch (start us, length us, event | category | flops | bytes accessed | tf_op | source)
XLA Modules:
  0.0 147.1 jit_solution(16628391991187976943)
XLA Ops:
  0.6 1.3 fusion.pick
  2.0 140.4 %shard_map.59 = (f32[384,1536]{1,0:T(8,128)}, f32[384,1536]{1,0:T(8,128)}) custom-call(bf16[64,256]{1,0:T(8,128)(2,1)} %fusion.pick, bf16[256,3072]{1,0:T(8,128)(2,1)} %bitcast.3, f32[384,1536]{1,0:T(8,128)} %tw_hbm.1, f32[384,1536]{1,0:T(8,128)} %sw_hbm.1), custom_call_target="tpu_custom_call" | custom-call | flops 7247757312 | bytes 16777216 | tf_op jit(solution)/shard_map/pallas_call | solution.py:477
  142.3 0.0 copy-start
  142.3 3.4 %copy.8 = f32[384,1536]{1,0:T(8,128)} copy(f32[384,1536]{1,0:T(8,128)} %get-tuple-element.4) | data formatting | bytes 4718592
  145.7 0.0 copy-done
  145.7 1.4 copy.9
Async XLA Ops:
  142.3 3.4 %copy-start = (f32[384,1536]{1,0:T(8,128)S(1)}, f32[384,1536]{1,0:T(8,128)}, u32[]{:S(2)}) copy-start(f32[384,1536]{1,0:T(8,128)} %get-tuple-element.5) | copy-start | bytes 7077892

commit v5 on v4

--- a/solution.py
+++ b/solution.py
@@ -124,7 +124,7 @@
     tile = 64
     fetched[0].wait()
     fetched[1].wait()
-    for q in range(blocks):
+    def panel_block(q):
         columns = slice(q * LANE_BLOCK, (q + 1) * LANE_BLOCK)
 
         @pl.loop(0, depth // tile)
@@ -136,6 +136,7 @@
             wt[q, z, rows, :] = following.astype(jnp.bfloat16)
             ws[q, rows, :] = student.astype(jnp.bfloat16)
 
+    def send_block(q):
         @pl.when(z > 0)
         def _():
             line_copy(0, q, 0, z, down).start()
@@ -144,8 +145,10 @@
         def _():
             line_copy(1, q, 0, z, up).start()
 
-    next_out = pltpu.make_async_copy(tnext, tnext_hbm, stores.at[blocks])
-    next_out.start()
+    early = blocks // 2
+    for q in range(early):
+        panel_block(q)
+        send_block(q)
 
     fetched[2].wait()
     lane = lax.broadcasted_iota(jnp.int32, (16, 128), 1)
@@ -161,6 +164,11 @@
 
     stats = remote(stat, stat_in, sts.at[0], str_.at[0], mirror)
     stats.start()
+
+    for q in range(early, blocks):
+        panel_block(q)
+    next_out = pltpu.make_async_copy(tnext, tnext_hbm, stores.at[blocks])
+    next_out.start()
 
     def pump(i, q):
         @pl.when(z + 1 + i < zs)
@@ -223,6 +231,8 @@
     mine = half_of(f)
     for j in range(1, n):
         swap_copy(j).start()
+    for q in range(early, blocks):
+        send_block(q)
     owned[mine, core, y, z] = pb[f]
     for j in range(1, 4):
         feature_copy(0, j).start()

time: 147 us -> 151 us (1.027)
  Pallas kernels: 140 us -> 144 us
    pallas_call x1, Pallas kernels: 140 us -> 144 us  [fused_shards(): pl.pallas_call(functools.partial(fused, n, keep * n), out_shape=(out, out...]
where the time goes in v5:
time: 151 us
  Pallas kernels  144 us (95%)
  local copies, waits for them, and re-layouts  4.78 us (3%)
    pallas_call x1, Pallas kernels, fused_shards(): pl.pallas_call(functools.partial(fused, n, keep * n), out_shape=(out, out...  144 us
    unnamed x4, local copies, waits for them, and re-layouts  4.78 us

profile of v5, /device:TPU:1, one launch (start us, length us, event | category | flops | bytes accessed | tf_op | source)
XLA Modules:
  0.0 151.2 jit_solution(10449510932771597240)
XLA Ops:
  0.6 1.3 fusion.pick
  2.0 144.5 %shard_map.59 = (f32[384,1536]{1,0:T(8,128)}, f32[384,1536]{1,0:T(8,128)}) custom-call(bf16[64,256]{1,0:T(8,128)(2,1)} %fusion.pick, bf16[256,3072]{1,0:T(8,128)(2,1)} %bitcast.3, f32[384,1536]{1,0:T(8,128)} %tw_hbm.1, f32[384,1536]{1,0:T(8,128)} %sw_hbm.1), custom_call_target="tpu_custom_call" | custom-call | flops 7247757312 | bytes 16777216 | tf_op jit(solution)/shard_map/pallas_call | solution.py:487
  146.5 0.0 copy-start
  146.5 3.4 %copy.8 = f32[384,1536]{1,0:T(8,128)} copy(f32[384,1536]{1,0:T(8,128)} %get-tuple-element.4) | data formatting | bytes 4718592
  149.8 0.0 copy-done
  149.8 1.4 copy.9
Async XLA Ops:
  146.5 3.4 %copy-start = (f32[384,1536]{1,0:T(8,128)S(1)}, f32[384,1536]{1,0:T(8,128)}, u32[]{:S(2)}) copy-start(f32[384,1536]{1,0:T(8,128)} %get-tuple-element.5) | copy-start | bytes 7077892

commit v6 on v4

--- a/solution.py
+++ b/solution.py
@@ -75,7 +75,7 @@
 LANE_BLOCK = 256
 
 
-def fused(n, total_kept, pick, images_hbm, tw_hbm, sw_hbm, tnext_hbm, grad_hbm, images, tw, sw, tnext, grad, stat, stat_in, nbuf, xk, wt, ws,
+def fused(n, total_kept, index, images_hbm, tw_hbm, sw_hbm, tnext_hbm, grad_hbm, pick, images, tw, sw, tnext, grad, stat, stat_in, nbuf, xk, wt, ws,
           pt, os_, or_, ys_, yr_, pb, pxs, owned, turned, pf, h1s, h1r, h2s, h2r, h3s, h3r, ebuf,
           sts, str_, xs, xr, ls, lr, ps, pr, as_, ar, ss, sr, h1ss, h1rs, h2ss, h2rs, h3ss, h3rs,
           oss, ors, yss, yrs, zss, zrs, ess, ers, bss, brs, loads, stores):
@@ -91,7 +91,7 @@
     patches, width = images.shape
     depth = tw.shape[0]
     blocks = tw.shape[1] // LANE_BLOCK
-    keep = pick.shape[0]
+    keep = index.shape[1]
     part = keep // 2
     sibling = (4 * z + 2 * y + other, t)
     across = (4 * z + 2 * (1 - y) + core, t)
@@ -113,6 +113,8 @@
     for j in range(4):
         pl.semaphore_signal(
             barrier, inc=1, device_id=(4 * z + lax.rem(spot + j, 4), 1 - t), device_id_type=MESH)
+    chosen = lax.broadcasted_iota(jnp.int32, (patches, keep), 0) == index[...]
+    pick[...] = jnp.where(chosen, 1.0, 0.0).T.astype(jnp.bfloat16)
     pl.semaphore_wait(barrier, n + 3)
 
     def line_copy(way, q, i, source, to):
@@ -254,9 +256,39 @@
     def h2_copy(q):
         return remote(h2s.at[q], h2r.at[q], h2ss.at[q], h2rs.at[q], across)
 
-    def level_copy(q, j):
-        to = lax.rem(z + j, zs)
-        return remote(h3s.at[q, to], h3r.at[q, j - 1], h3ss.at[q, j - 1], h3rs.at[q, j - 1], (4 * to + spot, t))
+    def chain_copy(way, q, e, to):
+        return remote(h3s.at[way, q, e], h3r.at[way, q, e], h3ss.at[way, q, e], h3rs.at[way, q, e], to)
+
+    def chain(q, way, first):
+        for e in range(zs):
+            ahead = e < z if way == 0 else e > z
+
+            @pl.when(ahead)
+            def _():
+                value = pf[q, :, y, e]
+                if not first:
+                    chain_copy(way, q, e, sibling).wait_recv()
+                    value = value + h3r[way, q, e].astype(jnp.float32)
+                h3s[way, q, e] = value.astype(jnp.bfloat16)
+                chain_copy(way, q, e, down if way == 0 else up).start()
+
+    def chain_step(q, hop):
+        if hop == 0:
+            @pl.when(z == zs - 1)
+            def _():
+                chain(q, 0, True)
+
+            @pl.when(z == 0)
+            def _():
+                chain(q, 1, True)
+        else:
+            @pl.when(z == zs - 1 - hop)
+            def _():
+                chain(q, 0, False)
+
+            @pl.when(z == hop)
+            def _():
+                chain(q, 1, False)
 
     @pl.loop(0, blocks)
     def _(q):
@@ -287,12 +319,15 @@
         @pl.loop(0, zs)
         def _(level):
             for g in range(2):
-                value = pf[q, g, y, level] + h2r[q, g, level].astype(jnp.float32)
-                pf[q, g, y, level] = value
-                h3s[q, level, g] = value.astype(jnp.bfloat16)
-
-        for j in range(1, zs):
-            level_copy(q, j).start()
+                pf[q, g, y, level] += h2r[q, g, level].astype(jnp.float32)
+
+        chain_step(q, 0)
+        for hop in range(1, zs - 1):
+            if q >= hop:
+                chain_step(q - hop, hop)
+    for late in range(1, zs - 1):
+        for hop in range(late, zs - 1):
+            chain_step(blocks - 1 + late - hop, hop)
 
     def feature_wait(plane, j):
         origin = lax.rem(spot + 4 - j, 4)
@@ -345,8 +380,11 @@
         pt[q, y] += or_[q, y]
 
     def error_of(q):
-        for j in range(1, zs):
-            level_copy(q, j).wait_recv()
+        for way in range(2):
+            @pl.when(z < zs - 1 if way == 0 else z > 0)
+            def _():
+                chain_copy(way, q, z, sibling).wait_recv()
+                pf[q, :, y, z] += h3r[way, q, z].astype(jnp.float32)
         across_copy(q).wait_recv()
         value = pt[q, y] + yr_[q].astype(jnp.float32)
         centre = jnp.sum(value, axis=0, keepdims=True) * (1.0 / patches)
@@ -358,8 +396,6 @@
         kept = (jnp.dot(pick[...], upper, preferred_element_type=jnp.float32)
                 + jnp.dot(pick[...], lower, preferred_element_type=jnp.float32))
         student = pf[q, :, y, z]
-        for j in range(1, zs):
-            student = student + h3r[q, j - 1].astype(jnp.float32)
         student = student.reshape(keep, LANE_BLOCK)
         ebuf[q, core, y, z] = ((student - kept) * (1.0 / math.sqrt(total_kept))).astype(jnp.bfloat16)
         for j in range(1, zs):
@@ -413,10 +449,14 @@
         sibling_copy(q).wait_send()
         across_copy(q).wait_send()
         for j in range(1, zs):
-            level_copy(q, j).wait_send()
             error_level(q, j).wait_send()
         error_across(q, y).wait_send()
         error_sibling(q, core).wait_send()
+        for e in range(zs):
+            for way in range(2):
+                @pl.when(e < z if way == 0 else e > z)
+                def _():
+                    chain_copy(way, q, e, sibling).wait_send()
     for j in range(1, n):
         swap_copy(j).wait_send()
     for j in range(1, 4):
@@ -431,11 +471,11 @@
     keep = keep_index.shape[1]
     depth, columns = teacher_weight.shape
     zs, blocks, part = n // 4, columns // LANE_BLOCK, keep // 2
-    pick = (keep_index[0][:, None] == jnp.arange(patches)[None, :]).astype(jnp.bfloat16)
     bf, fl = jnp.bfloat16, jnp.float32
     dma = pltpu.SemaphoreType.DMA
     vm = pltpu.VMEM
     scratch = [
+        vm((keep, patches), bf),
         vm((patches, width), bf), vm((depth, columns), fl), vm((depth, columns), fl),
         vm((depth, columns), fl), vm((depth, columns), fl),
         vm((patches, 128), fl), vm((patches, 128), fl),
@@ -457,8 +497,8 @@
         vm((blocks, 2, 2, zs, part, LANE_BLOCK), bf),
         vm((blocks, 2, zs, part, LANE_BLOCK), bf),
         vm((blocks, 2, zs, part, LANE_BLOCK), bf),
-        vm((blocks, zs, 2, part, LANE_BLOCK), bf),
-        vm((blocks, zs - 1, 2, part, LANE_BLOCK), bf),
+        vm((2, blocks, zs, 2, part, LANE_BLOCK), bf),
+        vm((2, blocks, zs, 2, part, LANE_BLOCK), bf),
         vm((blocks, 2, 2, zs, keep, LANE_BLOCK), bf),
         dma((1,)), dma((1,)),
         dma((2, 4)), dma((2, 4)),
@@ -467,7 +507,7 @@
         dma((n - 1,)), dma((n - 1,)),
         dma((1,)), dma((1,)),
         dma((blocks,)), dma((blocks,)), dma((blocks,)), dma((blocks,)),
-        dma((blocks, zs - 1)), dma((blocks, zs - 1)),
+        dma((2, blocks, zs)), dma((2, blocks, zs)),
         dma((blocks,)), dma((blocks,)), dma((blocks,)), dma((blocks,)),
         dma((blocks, zs - 1)), dma((blocks, zs - 1)),
         dma((blocks,)), dma((blocks,)), dma((blocks,)), dma((blocks,)),
@@ -484,7 +524,7 @@
             collective_id=0, has_side_effects=True, vmem_limit_bytes=60 * 2**20),
         cost_estimate=pl.CostEstimate(
             flops=2 * n * depth * columns * (patches + 2 * keep), bytes_accessed=2**24, transcendentals=0),
-    )(pick, images[0], teacher_weight, student_weight)
+    )(keep_index, images[0], teacher_weight, student_weight)
 
 
 def solution(mesh):

time: 147 us -> 142 us (0.966)
  Pallas kernels: 140 us -> 137 us
    pallas_call x1, Pallas kernels: 140 us -> 137 us  [fused_shards(): pl.pallas_call(functools.partial(fused, n, keep * n), out_shape=(out, out...]
where the time goes in v6:
time: 142 us
  Pallas kernels  137 us (96%)
  local copies, waits for them, and re-layouts  4.78 us (3%)
    pallas_call x1, Pallas kernels, fused_shards(): pl.pallas_call(functools.partial(fused, n, keep * n), out_shape=(out, out...  137 us
    unnamed x4, local copies, waits for them, and re-layouts  4.78 us

profile of v6, /device:TPU:1, one launch (start us, length us, event | category | flops | bytes accessed | tf_op | source)
XLA Modules:
  0.0 142.0 jit_solution(3585956153010028084)
XLA Ops:
  0.6 136.5 %shard_map.59 = (f32[384,1536]{1,0:T(8,128)}, f32[384,1536]{1,0:T(8,128)}) custom-call(s32[1,64]{1,0:T(1,128)} %index.1, bf16[256,3072]{1,0:T(8,128)(2,1)} %bitcast.1, f32[384,1536]{1,0:T(8,128)} %tw_hbm.1, f32[384,1536]{1,0:T(8,128)} %sw_hbm.1), custom_call_target="tpu_custom_call" | custom-call | flops 7247757312 | bytes 16777216 | tf_op jit(solution)/shard_map/pallas_call | solution.py:517
  137.2 0.0 copy-start
  137.2 3.4 %copy.8 = f32[384,1536]{1,0:T(8,128)} copy(f32[384,1536]{1,0:T(8,128)} %get-tuple-element.4) | data formatting | bytes 4718592
  140.5 0.0 copy-done
  140.5 1.4 copy.9
Async XLA Ops:
  137.2 3.4 %copy-start = (f32[384,1536]{1,0:T(8,128)S(1)}, f32[384,1536]{1,0:T(8,128)}, u32[]{:S(2)}) copy-start(f32[384,1536]{1,0:T(8,128)} %get-tuple-element.5) | copy-start | bytes 7077892

commit v7 on v6

--- a/solution.py
+++ b/solution.py
@@ -301,6 +301,9 @@
                       preferred_element_type=jnp.float32)
         pf[q] = own.reshape(split)
 
+    for q in range(blocks // 2):
+        pump(1, q)
+
     @pl.loop(0, blocks)
     def _(q):
         h1_copy(q).wait_recv()
@@ -313,7 +316,8 @@
         turned[g] = owned[g].reshape(rows_core, depth).T
 
     for q in range(blocks):
-        pump(1, q)
+        if q >= blocks // 2:
+            pump(1, q)
         h2_copy(q).wait_recv()
 
         @pl.loop(0, zs)
@@ -425,11 +429,18 @@
         columns = pl.ds(q * LANE_BLOCK, LANE_BLOCK)
         return pltpu.make_async_copy(grad.at[:, columns], grad_hbm.at[:, columns], stores.at[q])
 
-    stages = ((product, 0), (error_of, 1), (cores_add, 0), (levels_in, 2), (across_in, 3), (finish, 4))
-    for wave in range(blocks + 4):
+    stages = ((product, 0), (error_of, 1), (cores_add, 0), (levels_in, 2), (across_in, 3))
+    for wave in range(blocks + 3):
         for stage, lag in stages:
             if 0 <= wave - lag < blocks:
                 stage(wave - lag)
+        if wave == blocks:
+            for q in range(blocks - 3):
+                finish(q)
+        if wave > blocks:
+            finish(wave - 4)
+    for q in range(blocks - 1, blocks):
+        finish(q)
 
     for copy in (stats, kept_out, halves):
         copy.wait_send()

time: 142 us -> 142 us (level)
  no operation moved by 1% of the time
where the time goes in v7:
time: 142 us
  Pallas kernels  136 us (96%)
  local copies, waits for them, and re-layouts  4.78 us (3%)
    pallas_call x1, Pallas kernels, fused_shards(): pl.pallas_call(functools.partial(fused, n, keep * n), out_shape=(out, out...  136 us
    unnamed x4, local copies, waits for them, and re-layouts  4.78 us

profile of v7, /device:TPU:1, one launch (start us, length us, event | category | flops | bytes accessed | tf_op | source)
XLA Modules:
  0.0 141.9 jit_solution(10496628789169833236)
XLA Ops:
  0.6 136.5 %shard_map.59 = (f32[384,1536]{1,0:T(8,128)}, f32[384,1536]{1,0:T(8,128)}) custom-call(s32[1,64]{1,0:T(1,128)} %index.1, bf16[256,3072]{1,0:T(8,128)(2,1)} %bitcast.1, f32[384,1536]{1,0:T(8,128)} %tw_hbm.1, f32[384,1536]{1,0:T(8,128)} %sw_hbm.1), custom_call_target="tpu_custom_call" | custom-call | flops 7247757312 | bytes 16777216 | tf_op jit(solution)/shard_map/pallas_call | solution.py:528
  137.1 0.0 copy-start
  137.1 3.4 %copy.8 = f32[384,1536]{1,0:T(8,128)} copy(f32[384,1536]{1,0:T(8,128)} %get-tuple-element.4) | data formatting | bytes 4718592
  140.5 0.0 copy-done
  140.5 1.4 copy.9
Async XLA Ops:
  137.1 3.4 %copy-start = (f32[384,1536]{1,0:T(8,128)S(1)}, f32[384,1536]{1,0:T(8,128)}, u32[]{:S(2)}) copy-start(f32[384,1536]{1,0:T(8,128)} %get-tuple-element.5) | copy-start | bytes 7077892

commit v8 on v7

--- a/solution.py
+++ b/solution.py
@@ -315,9 +315,7 @@
     for g in range(2):
         turned[g] = owned[g].reshape(rows_core, depth).T
 
-    for q in range(blocks):
-        if q >= blocks // 2:
-            pump(1, q)
+    def student(q):
         h2_copy(q).wait_recv()
 
         @pl.loop(0, zs)
@@ -326,12 +324,18 @@
                 pf[q, g, y, level] += h2r[q, g, level].astype(jnp.float32)
 
         chain_step(q, 0)
+
+    def hops(q):
         for hop in range(1, zs - 1):
-            if q >= hop:
+            if 0 <= q - hop < blocks:
                 chain_step(q - hop, hop)
-    for late in range(1, zs - 1):
-        for hop in range(late, zs - 1):
-            chain_step(blocks - 1 + late - hop, hop)
+
+    ahead = blocks // 2
+    for q in range(ahead):
+        if ahead + q < blocks:
+            pump(1, ahead + q)
+        student(q)
+        hops(q)
 
     def feature_wait(plane, j):
         origin = lax.rem(spot + 4 - j, 4)
@@ -434,6 +438,10 @@
         for stage, lag in stages:
             if 0 <= wave - lag < blocks:
                 stage(wave - lag)
+            if stage is product:
+                if wave + ahead < blocks:
+                    student(wave + ahead)
+                hops(wave + ahead)
         if wave == blocks:
             for q in range(blocks - 3):
                 finish(q)

time: 142 us -> 138 us (0.972)
  Pallas kernels: 136 us -> 133 us
    pallas_call x1, Pallas kernels: 136 us -> 133 us  [fused_shards(): pl.pallas_call(functools.partial(fused, n, keep * n), out_shape=(out, out...]
where the time goes in v8:
time: 138 us
  Pallas kernels  133 us (96%)
  local copies, waits for them, and re-layouts  4.78 us (3%)
    pallas_call x1, Pallas kernels, fused_shards(): pl.pallas_call(functools.partial(fused, n, keep * n), out_shape=(out, out...  133 us
    unnamed x4, local copies, waits for them, and re-layouts  4.78 us

profile of v8, /device:TPU:1, one launch (start us, length us, event | category | flops | bytes accessed | tf_op | source)
XLA Modules:
  0.0 138.0 jit_solution(5747556676859123938)
XLA Ops:
  0.6 132.6 %shard_map.59 = (f32[384,1536]{1,0:T(8,128)}, f32[384,1536]{1,0:T(8,128)}) custom-call(s32[1,64]{1,0:T(1,128)} %index.1, bf16[256,3072]{1,0:T(8,128)(2,1)} %bitcast.1, f32[384,1536]{1,0:T(8,128)} %tw_hbm.1, f32[384,1536]{1,0:T(8,128)} %sw_hbm.1), custom_call_target="tpu_custom_call" | custom-call | flops 7247757312 | bytes 16777216 | tf_op jit(solution)/shard_map/pallas_call | solution.py:536
  133.3 0.0 copy-start
  133.3 3.4 %copy.8 = f32[384,1536]{1,0:T(8,128)} copy(f32[384,1536]{1,0:T(8,128)} %get-tuple-element.4) | data formatting | bytes 4718592
  136.6 0.0 copy-done
  136.6 1.4 %copy.9 = f32[384,1536]{1,0:T(8,128)} copy(f32[384,1536]{1,0:T(8,128)S(1)} %copy-done) | data formatting | bytes 4718592
Async XLA Ops:
  133.3 3.4 %copy-start = (f32[384,1536]{1,0:T(8,128)S(1)}, f32[384,1536]{1,0:T(8,128)}, u32[]{:S(2)}) copy-start(f32[384,1536]{1,0:T(8,128)} %get-tuple-element.5) | copy-start | bytes 7077892
